TPU v7x, 256 devices: a whole 4x4x8 slice. The times are simulated.
256 devices in a mesh: row: 32 (over x, y, core), col: 8 (over z).
Axes of the slice: x: 4, y: 4, z: 8, core: 2. Of those that a mesh axis runs over, the one named last changes fastest.
Arguments:
- eigvec_rows: bfloat16 [16384, 65536], P('row', 'col'), may hold values from -6 to 6
- split: int32 [2], replicated, may hold values from 0 to 8191
- shifts: float32 [2, 65536], P(None, 'col'), as said below
- roots: float32 [128], replicated, as said below
- deflate_mask: int32 [2, 65536], P(None, 'col'), may hold values from 0 to 1
- panel_source: int32 [128], replicated, may hold values from 0 to 131071, as said below
Outputs:
- panel: float32 [128, 16384], P('col', 'row')
Inputs may be any that keep to these rules, and one draw needn't show every extreme that they name: `shifts`: eigenvalues lie at least 0.02 from every secular root. `roots`: each root lies within 0.1 of an integer plus one half. `panel_source`: distinct indices; some are deflated and some are not.
All inputs are finite; a program needn't handle non-finite values.
Results may differ from a plain program's by a relative error of at most 0.002.
Values may be sent and summed in bfloat16 or wider, within the bound.
No kernel may reach another device: no remote copies, remote signals or barrier semaphores. Data moves between devices by JAX's collectives and lax.ppermute only.
A program may use at most 64 MiB of HBM per device.

v0:
```python
import jax
import jax.numpy as jnp
from jax import lax
from jax.sharding import PartitionSpec as P


def partner(x, axis, distance):
    return lax.ppermute(x, axis, [(i, i ^ 1 << distance) for i in range(lax.axis_size(axis))])


def local(eigvec_rows, split, shifts, roots, deflate_mask, panel_source):
    local_rows = eigvec_rows.shape[0]
    block_width = eigvec_rows.shape[1]
    row_count = lax.axis_size("row")
    col_count = lax.axis_size("col")
    half_devices = row_count // 2
    row_index = lax.axis_index("row")
    col_index = lax.axis_index("col")
    half_index = row_index // half_devices
    position = row_index % half_devices
    own_split = jnp.where(half_index == 0, split[0], split[1])
    holder = position == own_split // local_rows
    own_row = lax.dynamic_index_in_dim(eigvec_rows, own_split % local_rows, 0, keepdims=False)
    candidate = jnp.where(holder, own_row, jnp.zeros_like(own_row))
    for bit_number in range(half_devices.bit_length() - 1):
        candidate = candidate + partner(candidate, "row", bit_number)
    coupling = candidate.astype(jnp.float32)
    own_mask = lax.dynamic_index_in_dim(deflate_mask, half_index, 0, keepdims=False)
    own_shifts = lax.dynamic_index_in_dim(shifts, half_index, 0, keepdims=False)
    kept = jnp.where(own_mask == 1, jnp.float32(0.0), coupling)
    cauchy = kept[:, None] / (own_shifts[:, None] - roots[None, :])
    partial_norm = jnp.sum(cauchy * cauchy, axis=0)
    global_index = (
        half_index * (block_width * col_count)
        + col_index * block_width
        + jnp.arange(block_width, dtype=jnp.int32)
    )
    matches = global_index[:, None] == panel_source[None, :]
    partial_flag = jnp.sum(jnp.where(matches, own_mask[:, None], 0), axis=0).astype(jnp.float32)
    partials = jnp.stack([partial_norm, partial_flag])
    block_sums = lax.psum(partials, "col")
    totals = block_sums + partner(block_sums, "row", row_count.bit_length() - 2)
    norm2 = totals[0]
    deflated = totals[1] > 0.5
    merged = jnp.where(
        deflated[None, :], matches.astype(jnp.float32), cauchy / jnp.sqrt(norm2)[None, :]
    ).astype(jnp.bfloat16)
    return lax.psum_scatter(
        lax.dot_general(
            merged, eigvec_rows, (((0,), (1,)), ((), ())), preferred_element_type=jnp.float32
        ),
        "col",
        scatter_dimension=0,
        tiled=True,
    )


def solution(mesh):
    return jax.shard_map(
        local,
        mesh=mesh,
        in_specs=(P("row", "col"), P(), P(None, "col"), P(), P(None, "col"), P()),
        out_specs=P("col", "row"),
        check_vma=False,
    )
```

profile of v0, /device:TPU:8, one launch (start us, length us, event | category | flops | bytes accessed | tf_op | source)
XLA Modules:
  0.0 107.4 jit_solution(16329260404502226308)
XLA Ops:
  6.5 0.0 copy-start
  6.5 0.0 reduce-scatter.2.cloned.1.call-start
  6.5 1.3 %fusion.16 = (s32[1]{0:T(128)}, s32[1]{0:T(128)}) fusion(s32[2]{0:T(128)} %param.7), kind=kLoop, calls=%fused_computation.28 | loop fusion | bytes 16 | tf_op jit(solution)/shard_map/slice | solution.py:21
  9.2 1.0 fusion.15
  10.3 0.1 collective-permute-start
  10.4 0.0 copy-done
  10.4 0.9 constant_dynamic-slice_fusion.1
  11.3 0.2 collective-permute-done
  11.6 2.3 %collective-permute-start.1 = (bf16[8192]{0:T(1024)(128)(2,1)S(1)}, bf16[8192]{0:T(1024)(128)(2,1)S(1)}, u32[]{:S(2)}, u32[]{:S(2)}) collective-permute-start(bf16[8192]{0:T(1024)(128)(2,1)S(1)} %add.55), channel_id=1, source_target_pairs={{0,16},{8,24},{16,0},{24,8},{32,48},{40,56},{48,32},{56,40},{64,80... | collective-permute-start | bytes 49160 | tf_op jit(solution)/shard_map/ppermute | solution.py:8
  13.8 1.7 %collective-permute-done.1 = bf16[8192]{0:T(1024)(128)(2,1)S(1)} collective-permute-done((bf16[8192]{0:T(1024)(128)(2,1)S(1)}, bf16[8192]{0:T(1024)(128)(2,1)S(1)}, u32[]{:S(2)}, u32[]{:S(2)}) %collective-permute-start.1) | collective-permute-done | bytes 16416 | tf_op jit(solution)/shard_map/ppermute | solution.py:8
  15.5 2.2 %collective-permute-start.2 = (bf16[8192]{0:T(1024)(128)(2,1)S(1)}, bf16[8192]{0:T(1024)(128)(2,1)S(1)}, u32[]{:S(2)}, u32[]{:S(2)}) collective-permute-start(bf16[8192]{0:T(1024)(128)(2,1)S(1)} %add.56), channel_id=1, source_target_pairs={{0,32},{8,40},{16,48},{24,56},{32,0},{40,8},{48,16},{56,24},{64,96... | collective-permute-start | bytes 49160 | tf_op jit(solution)/shard_map/ppermute | solution.py:8
  17.8 3.4 %fusion.2 = s32[128]{0:T(128)S(1)} fusion(s32[8192]{0:T(1024)S(1)} %bitcast.12, s32[128]{0:T(128)} %param.11, s32[8192]{0:T(1024)S(1)} %iota_add_fusion), kind=kLoop, calls=%fused_computation.6 | loop fusion | flops 3145600 | bytes 66560 | tf_op jit(solution)/shard_map/reduce_sum | solution.py:39
  21.2 0.0 collective-permute-done.2
  21.2 1.6 %collective-permute-start.3 = (bf16[8192]{0:T(1024)(128)(2,1)S(1)}, bf16[8192]{0:T(1024)(128)(2,1)S(1)}, u32[]{:S(2)}, u32[]{:S(2)}) collective-permute-start(bf16[8192]{0:T(1024)(128)(2,1)S(1)} %add.57), channel_id=1, source_target_pairs={{0,64},{8,72},{16,80},{24,88},{32,96},{40,104},{48,112},{56,120},{... | collective-permute-start | bytes 49160 | tf_op jit(solution)/shard_map/ppermute | solution.py:8
  22.8 2.2 %collective-permute-done.3 = bf16[8192]{0:T(1024)(128)(2,1)S(1)} collective-permute-done((bf16[8192]{0:T(1024)(128)(2,1)S(1)}, bf16[8192]{0:T(1024)(128)(2,1)S(1)}, u32[]{:S(2)}, u32[]{:S(2)}) %collective-permute-start.3) | collective-permute-done | bytes 16416 | tf_op jit(solution)/shard_map/ppermute | solution.py:8
  25.1 5.2 %fusion.1 = f32[128]{0:T(128)S(1)} fusion(f32[128]{0:T(128)} %param.9, f32[8192]{0:T(1024)S(1)} %bitcast.14, f32[8192]{0:T(1024)S(1)} %convert_select_fusion), kind=kLoop, calls=%fused_computation.5 | loop fusion | flops 4194176 | bytes 66560 | tf_op jit(solution)/shard_map/reduce_sum | solution.py:32
  30.3 20.0 %psum.7 = f32[2,128]{1,0:T(2,128)S(1)} all-reduce(f32[2,128]{1,0:T(2,128)S(1)} %pad_maximum_fusion), channel_id=1, replica_groups=mesh['row'=32,'col'=8] {'col'}, use_global_device_ids=true, to_apply=%region_2.3 | all-reduce | flops 256 | bytes 2048 | tf_op jit(solution)/shard_map/psum | solution.py:41
  50.3 3.1 %collective-permute-start.4 = (f32[2,128]{1,0:T(2,128)S(1)}, f32[2,128]{1,0:T(2,128)S(1)}, u32[]{:S(2)}, u32[]{:S(2)}) collective-permute-start(f32[2,128]{1,0:T(2,128)S(1)} %psum.7), channel_id=1, source_target_pairs={{0,128},{8,136},{16,144},{24,152},{32,160},{40,168},{48,176},{56,1... | collective-permute-start | bytes 3080 | tf_op jit(solution)/shard_map/ppermute | solution.py:8
  53.4 2.0 %collective-permute-done.4 = f32[2,128]{1,0:T(2,128)S(1)} collective-permute-done((f32[2,128]{1,0:T(2,128)S(1)}, f32[2,128]{1,0:T(2,128)S(1)}, u32[]{:S(2)}, u32[]{:S(2)}) %collective-permute-start.4) | collective-permute-done | bytes 1056 | tf_op jit(solution)/shard_map/ppermute | solution.py:8
  55.4 10.7 %fusion.6 = f32[128,512]{1,0:T(8,128)} fusion(bf16[512,8192]{1,0:T(8,128)(2,1)} %param.6, f32[128]{0:T(128)S(1)} %sqrt_bitcast_fusion, s32[128]{0:T(128)} %param.11, f32[128]{0:T(128)} %param.9, f32[8192]{0:T(1024)S(1)} %bitcast.15, f32[8192]{0:T(1024)S(1)} %convert_select_fusion, s32[8192]{0:T(1024)S(1)} %iota_add_fusion, ...), kind=kOutput, calls=%fused_computation.10 | convolution fusion | flops 1081081856 | bytes 8750720 | tf_op jit(solution)/shard_map/dot_general | solution.py:49
  66.2 0.0 reduce-scatter.2.cloned.1.call-update
  66.2 34.4 %reduce-scatter.2.cloned.1.call-done = f32[16,512]{1,0:T(8,128)} async-done(((f32[128,512]{1,0:T(8,128)}), f32[16,512]{1,0:T(8,128)}) %reduce-scatter.2.cloned.1.call-update) | async-done | bytes 32784 | tf_op jit(solution)/shard_map/reduce_scatter | solution.py:48
  (11 shorter events, 0.1 us)
Async XLA Ops:
  6.5 3.8 %copy-start = (f32[2,8192]{1,0:T(2,128)S(1)}, f32[2,8192]{1,0:T(2,128)}, u32[]{:S(2)}) copy-start(f32[2,8192]{1,0:T(2,128)} %param.8) | copy-start | bytes 196612
  6.5 94.0 %reduce-scatter.2.cloned.1.call-start = ((), (), s32[]{:S(2)}) async-start(), calls=%async_computation.1 | async-start | bytes 294912 | tf_op jit(solution)/shard_map/reduce_scatter | solution.py:48
  10.3 1.3 %collective-permute-start = (bf16[8192]{0:T(1024)(128)(2,1)S(1)}, bf16[8192]{0:T(1024)(128)(2,1)S(1)}, u32[]{:S(2)}, u32[]{:S(2)}) collective-permute-start(bf16[8192]{0:T(1024)(128)(2,1)S(1)} %fusion.15), channel_id=1, source_target_pairs={{0,8},{8,0},{16,24},{24,16},{32,40},{40,32},{48,56},{56,48},{64,72... | collective-permute-start | bytes 49160 | tf_op jit(solution)/shard_map/ppermute | solution.py:8
  11.6 4.0 %collective-permute-start.1 = (bf16[8192]{0:T(1024)(128)(2,1)S(1)}, bf16[8192]{0:T(1024)(128)(2,1)S(1)}, u32[]{:S(2)}, u32[]{:S(2)}) collective-permute-start(bf16[8192]{0:T(1024)(128)(2,1)S(1)} %add.55), channel_id=1, source_target_pairs={{0,16},{8,24},{16,0},{24,8},{32,48},{40,56},{48,32},{56,40},{64,80... | collective-permute-start | bytes 49160 | tf_op jit(solution)/shard_map/ppermute | solution.py:8
  15.5 5.7 %collective-permute-start.2 = (bf16[8192]{0:T(1024)(128)(2,1)S(1)}, bf16[8192]{0:T(1024)(128)(2,1)S(1)}, u32[]{:S(2)}, u32[]{:S(2)}) collective-permute-start(bf16[8192]{0:T(1024)(128)(2,1)S(1)} %add.56), channel_id=1, source_target_pairs={{0,32},{8,40},{16,48},{24,56},{32,0},{40,8},{48,16},{56,24},{64,96... | collective-permute-start | bytes 49160 | tf_op jit(solution)/shard_map/ppermute | solution.py:8
  21.2 3.8 %collective-permute-start.3 = (bf16[8192]{0:T(1024)(128)(2,1)S(1)}, bf16[8192]{0:T(1024)(128)(2,1)S(1)}, u32[]{:S(2)}, u32[]{:S(2)}) collective-permute-start(bf16[8192]{0:T(1024)(128)(2,1)S(1)} %add.57), channel_id=1, source_target_pairs={{0,64},{8,72},{16,80},{24,88},{32,96},{40,104},{48,112},{56,120},{... | collective-permute-start | bytes 49160 | tf_op jit(solution)/shard_map/ppermute | solution.py:8
  50.3 5.1 %collective-permute-start.4 = (f32[2,128]{1,0:T(2,128)S(1)}, f32[2,128]{1,0:T(2,128)S(1)}, u32[]{:S(2)}, u32[]{:S(2)}) collective-permute-start(f32[2,128]{1,0:T(2,128)S(1)} %psum.7), channel_id=1, source_target_pairs={{0,128},{8,136},{16,144},{24,152},{32,160},{40,168},{48,176},{56,1... | collective-permute-start | bytes 3080 | tf_op jit(solution)/shard_map/ppermute | solution.py:8
Sparse Core Ops, SparseCore 0:
  66.3 34.2 reduce-scatter.1
where the time goes:
time: 108 us; the launch traced here: 107 us
  waiting for transfers between devices  40.6 us (38%)
  blocking collectives  20 us (19%)
  between operations  14.9 us (14%)
  matrix products  10.7 us (10%)
  other arithmetic  9.72 us (9%)
  starting transfers between devices  9.24 us (9%)
  local copies, waits for them, and re-layouts  2.24 us (2%)
    reduce_scatter x1, waiting for transfers between devices, local(): lax.psum_scatter(lax.dot_general(merged, eigvec_rows, (((0,), (1,)), ((),...  34.4 us
    psum x1, blocking collectives, local(): block_sums = lax.psum(partials, 'col')  20 us
    dot_general x1, matrix products, local(): lax.dot_general(merged, eigvec_rows, (((0,), (1,)), ((), ())), preferred_...  10.7 us
    ppermute x5, starting transfers between devices, partner(): lax.ppermute(x, axis, [(i, i ^ 1 << distance) for i in range(lax.axis_siz...  9.24 us
    ppermute x5, waiting for transfers between devices, partner(): lax.ppermute(x, axis, [(i, i ^ 1 << distance) for i in range(lax.axis_siz...  6.23 us
    reduce_sum x1, other arithmetic, local(): partial_norm = jnp.sum(cauchy * cauchy, axis=0)  5.19 us
    reduce_sum x1, other arithmetic, local(): jnp.sum(jnp.where(matches, own_mask[:, None], 0), axis=0)  3.44 us
  transfers between devices with their start and end apart: 6, of which 5 were waited for; matrix products, arithmetic and copies ran while one was open for 4% of the time, Pallas kernels for 0%

commit v1 on v0

v1 whole, which is shorter than its diff:
```python
import functools

import jax
import jax.numpy as jnp
from jax import lax
from jax.experimental import pallas as pl
from jax.experimental.pallas import tpu as pltpu
from jax.sharding import PartitionSpec as P

LANES = 128
PIECE = 512
ALIGN = 16


def pick_kernel(split_ref, rows_ref, out_ref, window, sem, *, height):
    half = lax.axis_index("row") // (lax.axis_size("row") // 2)
    row = split_ref[half] % height
    base = pl.multiple_of((row // ALIGN) * ALIGN, ALIGN)
    copy = pltpu.make_async_copy(rows_ref.at[pl.ds(base, ALIGN)], window, sem)
    copy.start()
    copy.wait()
    inner = lax.broadcasted_iota(jnp.int32, (ALIGN, PIECE), 0) == row - base
    pieces = []
    for start in range(0, window.shape[1], PIECE):
        block = window[:, pl.ds(start, PIECE)].astype(jnp.float32)
        pieces.append(jnp.sum(jnp.where(inner, block, 0.0), axis=0, keepdims=True))
    line = jnp.concatenate(pieces, axis=0).astype(out_ref.dtype)
    for target in range(out_ref.shape[0]):
        out_ref[target] = line


def spread(line):
    return jnp.broadcast_to(line, (LANES, line.shape[1])).T


def merge_kernel(
    split_ref, line_ref, shifts_ref, mask_ref, roots_ref, source_ref, split_out, sums_ref,
    mask_line, kept_line, shift_line, *, height, width, columns
):
    row = lax.axis_index("row")
    half = row // (lax.axis_size("row") // 2)
    col = lax.axis_index("col")
    panel = roots_ref.shape[1]
    holder = split_ref[half] // height
    own = lambda ref, at: jnp.where(half == 0, ref[0:1, at], ref[1:2, at])
    local = source_ref[...] - (half * columns + col * width)
    here = (local >= 0) & (local < width)
    local = jnp.where(here, local, -1)
    local_all = spread(local)
    lane = lax.broadcasted_iota(jnp.int32, (panel, LANES), 1)
    tiles = width // LANES

    line = line_ref[holder].astype(jnp.float32)
    for a in range(width // PIECE):
        at = slice(a * PIECE, (a + 1) * PIECE)
        mask = own(mask_ref, at)
        mask_line[:, at] = mask
        kept_line[:, at] = jnp.where(mask == 1, 0.0, line[a : a + 1])
        shift_line[:, at] = own(shifts_ref, at)

    def count(t, flags):
        mask = mask_line[:, pl.ds(pl.multiple_of(t * LANES, LANES), LANES)]
        return flags + jnp.where((local_all == lane + t * LANES) & (mask == 1), 1.0, 0.0)

    flags = lax.fori_loop(0, tiles, count, jnp.zeros((panel, LANES), jnp.float32), unroll=4)
    flag = jnp.sum(flags, axis=1, keepdims=True)
    roots_all = jnp.where(flag > 0.5, 3e38, spread(roots_ref[...]))
    unit_all = jnp.where(flag > 0.5, local_all, -1)

    def body(t, norm):
        at = pl.ds(pl.multiple_of(t * LANES, LANES), LANES)
        cauchy = kept_line[:, at] / (shift_line[:, at] - roots_all)
        value = jnp.where(unit_all == lane + t * LANES, 1.0, cauchy)
        high = value.astype(jnp.bfloat16)
        split_out[0:panel, at] = high
        split_out[panel : 2 * panel, at] = (value - high.astype(jnp.float32)).astype(jnp.bfloat16)
        return norm + cauchy * cauchy

    norm = lax.fori_loop(0, tiles, body, jnp.zeros((panel, LANES), jnp.float32), unroll=4)
    total = jnp.sum(norm, axis=1, keepdims=True)
    position = lax.broadcasted_iota(jnp.int32, (panel, LANES), 1)
    sums_ref[...] = jnp.where(position == 0, total, jnp.where(position == 1, flag, 0.0))


def product_kernel(split_in, rows_ref, sums_ref, other_ref, out_ref):
    panel = sums_ref.shape[0]
    groups, per_group, _ = out_ref.shape
    height = rows_ref.shape[0]
    both = lax.dot_general(
        split_in[...], rows_ref[...], (((1,), (1,)), ((), ())), preferred_element_type=jnp.float32
    )
    out = both[0:panel] + both[panel : 2 * panel]
    own = sums_ref[...]
    other = other_ref[...]
    lane = lax.broadcasted_iota(jnp.int32, own.shape, 1)
    extra = own + jnp.where(lane == 0, other, jnp.where(lane == 2, pltpu.roll(other, 1, 1), 0.0))
    out_ref[:, :, 0:height] = out.reshape(groups, per_group, height)
    out_ref[:, :, height:] = extra.reshape(groups, per_group, LANES)


def finish_kernel(parts_ref, out_ref):
    groups = parts_ref.shape[0]
    height = out_ref.shape[1]
    extra = parts_ref[:, :, height:]
    total = jnp.sum(extra, axis=0)
    norm2 = total[:, 0:1]
    deflated = total[:, 1:2] + total[:, 2:3] > 0.5
    scale = 1.0 / jnp.sqrt(norm2)
    result = jnp.zeros(out_ref.shape, jnp.float32)
    for group in range(groups):
        weight = jnp.where(deflated, extra[group, :, 1:2], scale)
        result = result + weight * parts_ref[group, :, 0:height]
    out_ref[...] = jnp.where(deflated & (total[:, 1:2] < 0.5), 0.0, result)


def local(eigvec_rows, split, shifts, roots, deflate_mask, panel_source):
    height, width = eigvec_rows.shape
    row_count = lax.axis_size("row")
    col_count = lax.axis_size("col")
    half_devices = row_count // 2
    panel = roots.shape[0]
    vmem = pl.BlockSpec(memory_space=pltpu.VMEM)
    smem = pl.BlockSpec(memory_space=pltpu.SMEM)
    anywhere = pl.BlockSpec(memory_space=pl.ANY)
    lines = pl.pallas_call(
        functools.partial(pick_kernel, height=height),
        out_shape=jax.ShapeDtypeStruct((half_devices, width // PIECE, PIECE), eigvec_rows.dtype),
        in_specs=[smem, anywhere],
        out_specs=vmem,
        scratch_shapes=[pltpu.VMEM((ALIGN, width), eigvec_rows.dtype), pltpu.SemaphoreType.DMA],
        name="pick_line",
    )(split, eigvec_rows)
    halves = [list(range(half_devices)), list(range(half_devices, row_count))]
    lines = lax.all_to_all(lines, "row", 0, 0, axis_index_groups=halves)
    split_merged, sums = pl.pallas_call(
        functools.partial(merge_kernel, height=height, width=width, columns=width * col_count),
        out_shape=(
            jax.ShapeDtypeStruct((2 * panel, width), jnp.bfloat16),
            jax.ShapeDtypeStruct((panel, LANES), jnp.float32),
        ),
        in_specs=[smem, vmem, vmem, vmem, vmem, vmem],
        out_specs=(vmem, vmem),
        scratch_shapes=[pltpu.VMEM((1, width), kind) for kind in (jnp.int32, jnp.float32, jnp.float32)],
        compiler_params=pltpu.CompilerParams(vmem_limit_bytes=32 * 2**20),
        name="merge_columns",
    )(split, lines, shifts, deflate_mask, roots.reshape(1, -1), panel_source.reshape(1, -1))
    flip = half_devices + half_devices // 2
    other = lax.ppermute(sums, "row", [(i, i ^ flip) for i in range(row_count)])
    parts = pl.pallas_call(
        product_kernel,
        out_shape=jax.ShapeDtypeStruct((col_count, panel // col_count, height + LANES), jnp.float32),
        in_specs=[vmem, vmem, vmem, vmem],
        out_specs=vmem,
        compiler_params=pltpu.CompilerParams(vmem_limit_bytes=32 * 2**20),
        name="block_product",
    )(split_merged, eigvec_rows, sums, other)
    parts = lax.all_to_all(parts, "col", 0, 0)
    return pl.pallas_call(
        finish_kernel,
        out_shape=jax.ShapeDtypeStruct((panel // col_count, height), jnp.float32),
        in_specs=[vmem],
        out_specs=vmem,
        name="scale_and_add",
    )(parts)


def solution(mesh):
    return jax.shard_map(
        local,
        mesh=mesh,
        in_specs=(P("row", "col"), P(), P(None, "col"), P(), P(None, "col"), P()),
        out_specs=P("col", "row"),
        check_vma=False,
    )
```

time: 108 us -> 53.4 us (0.49)
  waiting for transfers between devices: 40.6 us -> 3.45 us
  between operations: 14.9 us -> 0.07 us
  blocking collectives: 20 us -> 33 us
  matrix products: 10.7 us -> 0 us
  Pallas kernels: 0 us -> 10.5 us
  other arithmetic: 9.72 us -> 0 us
  starting transfers between devices: 9.24 us -> 2.61 us
  local copies, waits for them, and re-layouts: 2.24 us -> 3.4 us
    reduce_scatter x1 -> x0, waiting for transfers between devices: 34.4 us -> none  [local(): lax.psum_scatter(lax.dot_general(merged, eigvec_rows, (((0,), (1,)), ((),...]
    all_to_all x0 -> x2, blocking collectives: none -> 33 us  [the longest x1 21.7 us: local(): parts = lax.all_to_all(parts, 'col', 0, 0)]
    psum x1 -> x0, blocking collectives: 20 us -> none  [local(): block_sums = lax.psum(partials, 'col')]
    dot_general x1 -> x0, matrix products: 10.7 us -> none  [local(): lax.dot_general(merged, eigvec_rows, (((0,), (1,)), ((), ())), preferred_...]
    pallas_call x0 -> x4, Pallas kernels: none -> 10.5 us  [the longest x1 3.78 us: local(): pl.pallas_call(functools.partial(merge_kernel, height=height, width=width...]
    reduce_sum x2 -> x0, other arithmetic: 8.64 us -> none  [the longest x1 5.19 us: local(): partial_norm = jnp.sum(cauchy * cauchy, axis=0)]
    ppermute x5 -> x1, starting transfers between devices: 9.24 us -> 2.61 us  [local(): other = lax.ppermute(sums, 'row', [(i, i ^ flip) for i in range(row_count)])]
    unnamed x2 -> x12, local copies, waits for them, and re-layouts: 0.01 us -> 3.4 us
  transfers between devices with their start and end apart: 6 -> 1, of which waited for: 5 -> 1; matrix products, arithmetic and copies ran while one was open for 4% -> 0% of each run, Pallas kernels for 0% -> 0%
where the time goes in v1:
time: 53.4 us; the launch traced here: 53.1 us
  blocking collectives  33 us (62%)
  Pallas kernels  10.5 us (20%)
  waiting for transfers between devices  3.45 us (6%)
  local copies, waits for them, and re-layouts  3.4 us (6%)
  starting transfers between devices  2.61 us (5%)
    all_to_all x1, blocking collectives, local(): parts = lax.all_to_all(parts, 'col', 0, 0)  21.7 us
    all_to_all x1, blocking collectives, local(): lines = lax.all_to_all(lines, 'row', 0, 0, axis_index_groups=halves)  11.3 us
    pallas_call x1, Pallas kernels, local(): pl.pallas_call(functools.partial(merge_kernel, height=height, width=width...  3.78 us
    ppermute x1, waiting for transfers between devices, local(): other = lax.ppermute(sums, 'row', [(i, i ^ flip) for i in range(row_count)])  3.45 us
    unnamed x12, local copies, waits for them, and re-layouts  3.4 us
    ppermute x1, starting transfers between devices, local(): other = lax.ppermute(sums, 'row', [(i, i ^ flip) for i in range(row_count)])  2.61 us
    pallas_call x1, Pallas kernels, local(): pl.pallas_call(functools.partial(pick_kernel, height=height), out_shape=j...  2.6 us
    pallas_call x1, Pallas kernels, local(): pl.pallas_call(product_kernel, out_shape=jax.ShapeDtypeStruct((col_count,...  2.35 us
  transfers between devices with their start and end apart: 1, of which 1 were waited for; matrix products, arithmetic and copies ran while one was open for 0% of the time, Pallas kernels for 0%

profile of v1, /device:TPU:8, one launch (start us, length us, event | category | flops | bytes accessed | tf_op | source)
XLA Modules:
  0.0 53.1 jit_solution(17298648356937417248)
XLA Ops:
  0.0 0.0 copy-start.3
  0.0 0.0 copy-start.5
  0.0 0.0 copy-start.2
  0.0 0.0 copy-start.4
  0.0 0.0 copy-start.1
  0.0 2.6 %pick_line.1 = bf16[16,16,512]{2,1,0:T(8,128)(2,1)} custom-call(s32[2]{0:T(128)} %split_ref.3, bf16[512,8192]{1,0:T(8,128)(2,1)} %rows_ref.3), custom_call_target="tpu_custom_call" | custom-call | tf_op jit(solution)/shard_map/pick_line/pallas_call | solution.py:125
  2.6 11.3 %all_to_all.10.line_ref = bf16[16,16,512]{2,1,0:T(8,128)(2,1)S(1)} all-to-all(bf16[16,16,512]{2,1,0:T(8,128)(2,1)} %pick_line.1), channel_id=1, replica_groups={{0,8,16,24,32,40,48,56,64,72,80,88,96,104,112,120},{128,136,144,152,160..., dimensions={0} | all-to-all | bytes 524288 | tf_op jit(solution)/shard_map/all_to_all | solution.py:134
  14.0 0.0 copy-done.3
  14.0 0.0 copy-done.5
  14.0 0.0 copy-done.2
  14.0 0.0 copy-done.4
  14.0 0.0 copy-done.1
  14.0 3.8 %merge_columns.1 = (bf16[256,8192]{1,0:T(8,128)(2,1)S(1)}, f32[128,128]{1,0:T(8,128)S(1)}) custom-call(s32[2]{0:T(128)S(1)} %copy-done.3, bf16[16,16,512]{2,1,0:T(8,128)(2,1)S(1)} %all_to_all.10.line_ref, f32[2,8192]{1,0:T(2,128)S(1)} %copy-done.1, s32[2,8192]{1,0:T(2,128)S(1)} %copy-done.2, f32[1,128]{1,0:T(1,128)S(1)} %bitcast.2, s32[1,128]{1,0:T(1,128)S(1)} %bitcast.3), custom_call_target="tpu_custom_call" | custom-call | tf_op jit(solution)/shard_map/merge_columns/pallas_call | solution.py:135
  17.8 2.6 %collective-permute-start = (f32[128,128]{1,0:T(8,128)S(1)}, f32[128,128]{1,0:T(8,128)S(1)}, u32[]{:S(2)}, u32[]{:S(2)}) collective-permute-start(f32[128,128]{1,0:T(8,128)S(1)} %get-tuple-element.8.sums_ref), channel_id=1, source_target_pairs={{0,192},{8,200},{16,208},{24,216},{32,224},{40,232},{48,240},{56,2... | collective-permute-start | bytes 196616 | tf_op jit(solution)/shard_map/ppermute | solution.py:148
  20.4 3.4 %collective-permute-done.other_ref = f32[128,128]{1,0:T(8,128)S(1)} collective-permute-done((f32[128,128]{1,0:T(8,128)S(1)}, f32[128,128]{1,0:T(8,128)S(1)}, u32[]{:S(2)}, u32[]{:S(2)}) %collective-permute-start) | collective-permute-done | bytes 65568 | tf_op jit(solution)/shard_map/ppermute | solution.py:148
  23.8 0.0 copy-start
  23.8 3.4 %copy-done = bf16[512,8192]{1,0:T(8,128)(2,1)S(1)} copy-done((bf16[512,8192]{1,0:T(8,128)(2,1)S(1)}, bf16[512,8192]{1,0:T(8,128)(2,1)}, u32[]{:S(2)}) %copy-start) | copy-done | bytes 8388632
  27.2 2.4 %block_product.1 = f32[8,16,640]{2,1,0:T(8,128)S(1)} custom-call(bf16[256,8192]{1,0:T(8,128)(2,1)S(1)} %get-tuple-element.7.split_in, bf16[512,8192]{1,0:T(8,128)(2,1)S(1)} %copy-done, f32[128,128]{1,0:T(8,128)S(1)} %get-tuple-element.8.sums_ref, f32[128,128]{1,0:T(8,128)S(1)} %collective-permute-done.other_ref), custom_call_target="tpu_custom_call" | custom-call | tf_op jit(solution)/shard_map/block_product/pallas_call | solution.py:149
  29.6 21.7 %all_to_all.11.parts_ref = f32[8,16,640]{2,1,0:T(8,128)} all-to-all(f32[8,16,640]{2,1,0:T(8,128)S(1)} %block_product.1), channel_id=1, replica_groups=mesh['row'=32,'col'=8] {'col'}, dimensions={0} | all-to-all | bytes 655360 | tf_op jit(solution)/shard_map/all_to_all | solution.py:157
  51.3 1.8 %scale_and_add.1 = f32[16,512]{1,0:T(8,128)} custom-call(f32[8,16,640]{2,1,0:T(8,128)} %all_to_all.11.parts_ref), custom_call_target="tpu_custom_call" | custom-call | tf_op jit(solution)/shard_map/scale_and_add/pallas_call | solution.py:158
Async XLA Ops:
  0.0 14.0 %copy-start.3 = (s32[2]{0:T(128)S(1)}, s32[2]{0:T(128)}, u32[]{:S(2)}) copy-start(s32[2]{0:T(128)} %split_ref.3) | copy-start | bytes 28
  0.0 14.0 %copy-start.5 = (s32[128]{0:T(128)S(1)}, s32[128]{0:T(128)}, u32[]{:S(2)}) copy-start(s32[128]{0:T(128)} %param.11) | copy-start | bytes 1540
  0.0 14.0 %copy-start.2 = (s32[2,8192]{1,0:T(2,128)S(1)}, s32[2,8192]{1,0:T(2,128)}, u32[]{:S(2)}) copy-start(s32[2,8192]{1,0:T(2,128)} %mask_ref.1) | copy-start | bytes 196612
  0.0 14.0 %copy-start.4 = (f32[128]{0:T(128)S(1)}, f32[128]{0:T(128)}, u32[]{:S(2)}) copy-start(f32[128]{0:T(128)} %param.9) | copy-start | bytes 1540
  0.0 14.0 %copy-start.1 = (f32[2,8192]{1,0:T(2,128)S(1)}, f32[2,8192]{1,0:T(2,128)}, u32[]{:S(2)}) copy-start(f32[2,8192]{1,0:T(2,128)} %shifts_ref.1) | copy-start | bytes 196612
  17.8 6.1 %collective-permute-start = (f32[128,128]{1,0:T(8,128)S(1)}, f32[128,128]{1,0:T(8,128)S(1)}, u32[]{:S(2)}, u32[]{:S(2)}) collective-permute-start(f32[128,128]{1,0:T(8,128)S(1)} %get-tuple-element.8.sums_ref), channel_id=1, source_target_pairs={{0,192},{8,200},{16,208},{24,216},{32,224},{40,232},{48,240},{56,2... | collective-permute-start | bytes 196616 | tf_op jit(solution)/shard_map/ppermute | solution.py:148
  23.8 3.4 %copy-start = (bf16[512,8192]{1,0:T(8,128)(2,1)S(1)}, bf16[512,8192]{1,0:T(8,128)(2,1)}, u32[]{:S(2)}) copy-start(bf16[512,8192]{1,0:T(8,128)(2,1)} %rows_ref.3) | copy-start | bytes 25165828

commit v2 on v1

v2 whole, which is shorter than its diff:
```python
import functools

import jax
import jax.numpy as jnp
from jax import lax
from jax.experimental import pallas as pl
from jax.experimental.pallas import tpu as pltpu
from jax.sharding import PartitionSpec as P

LANES = 128
PIECE = 512
ALIGN = 16
SUBLANES = 8


def pick_kernel(split_ref, rows_ref, out_ref, window, sem, *, height):
    half = lax.axis_index("row") // (lax.axis_size("row") // 2)
    row = split_ref[half] % height
    base = pl.multiple_of((row // ALIGN) * ALIGN, ALIGN)
    copy = pltpu.make_async_copy(rows_ref.at[pl.ds(base, ALIGN)], window, sem)
    copy.start()
    copy.wait()
    inner = row - base
    lower = inner < SUBLANES
    inner = lax.rem(inner, SUBLANES)
    sublane = lax.broadcasted_iota(jnp.int32, (SUBLANES, PIECE), 0)
    blocks = [jnp.zeros((SUBLANES, PIECE), jnp.float32) for _ in range(out_ref.shape[1] // SUBLANES)]
    for a in range(out_ref.shape[1]):
        both = window[:, a * PIECE : (a + 1) * PIECE].astype(jnp.float32)
        eight = jnp.where(lower, both[0:SUBLANES], both[SUBLANES:])
        target = a % SUBLANES
        turned = pltpu.roll(eight, lax.rem(target - inner + SUBLANES, SUBLANES), 0)
        blocks[a // SUBLANES] = jnp.where(sublane == target, turned, blocks[a // SUBLANES])
    line = jnp.concatenate(blocks, axis=0).astype(out_ref.dtype)
    for target in range(out_ref.shape[0]):
        out_ref[target] = line


def held_kernel(split_ref, lines_ref, out_ref, *, height):
    half = lax.axis_index("row") // (lax.axis_size("row") // 2)
    out_ref[...] = lines_ref[split_ref[half] // height]


def spread(line):
    return jnp.broadcast_to(line, (LANES, line.shape[1])).T


def line_of(half, ref, at):
    return jnp.where(half == 0, ref[0:1, at], ref[1:2, at])


def poles(half, line, mask_ref, shifts_ref, kept_line, shift_line):
    for a in range(line.shape[0]):
        at = slice(a * PIECE, (a + 1) * PIECE)
        kept_line[:, at] = jnp.where(line_of(half, mask_ref, at) == 1, 0.0, line[a : a + 1])
        shift_line[:, at] = line_of(half, shifts_ref, at)


def cauchy_tile(kept_line, shift_line, roots_all, at):
    gap = shift_line[:, at] - roots_all
    rough = pl.reciprocal(gap, approx=True)
    return (kept_line[:, at] * rough) * (2.0 - gap * rough)


def merge_kernel(
    split_ref, lines_ref, rows_ref, shifts_ref, mask_ref, roots_ref, source_ref,
    split_out, part_ref, sums_ref,
    mask_square, kept_line, shift_line, *, height, width, columns
):
    row = lax.axis_index("row")
    half = row // (lax.axis_size("row") // 2)
    col = lax.axis_index("col")
    panel = roots_ref.shape[1]
    first = part_ref.shape[1]
    tiles = width // LANES
    for h in range(2):
        for t in range(tiles):
            at = slice(t * LANES, (t + 1) * LANES)
            mask_square[h * tiles + t : h * tiles + t + 1, :] = mask_ref[h : h + 1, at].astype(jnp.float32)
    source = spread(source_ref[...])
    source_half = (source >= columns).astype(jnp.int32)
    local = source - source_half * columns - col * width
    here = (local >= 0) & (local < width)
    lane = lax.broadcasted_iota(jnp.int32, (panel, LANES), 1)
    tile_of = jnp.where(here, source_half * tiles + local // LANES, -1)
    picked = jnp.dot(
        jnp.where(lane == tile_of, 1.0, 0.0).astype(jnp.bfloat16),
        mask_square[...].astype(jnp.bfloat16),
        preferred_element_type=jnp.float32,
    )
    deflated = jnp.sum(jnp.where(lane == local % LANES, picked, 0.0), axis=1, keepdims=True) > 0.5
    own_flag = deflated & (source_half == half)
    roots_all = jnp.where(own_flag, 3e38, spread(roots_ref[...]))
    unit_all = jnp.where(own_flag, local, -1)
    line = lines_ref[split_ref[half] // height].astype(jnp.float32)
    poles(half, line, mask_ref, shifts_ref, kept_line, shift_line)
    first_lane = lax.broadcasted_iota(jnp.int32, (1, LANES), 1)

    def fill(t, norm):
        at = pl.ds(pl.multiple_of(t * LANES, LANES), LANES)
        cauchy = cauchy_tile(kept_line, shift_line, roots_all, at)
        value = jnp.where(unit_all == first_lane + t * LANES, 1.0, cauchy)
        high = value.astype(jnp.bfloat16)
        split_out[0:panel, at] = high
        split_out[panel : 2 * panel, at] = (value - high.astype(jnp.float32)).astype(jnp.bfloat16)
        return norm + cauchy * cauchy

    norm = lax.fori_loop(0, tiles, fill, jnp.zeros((panel, LANES), jnp.float32), unroll=4)
    total = lax.dot_general(
        split_out[...], rows_ref[0:first], (((1,), (1,)), ((), ())), preferred_element_type=jnp.float32
    )
    part_ref[...] = total[0:panel] + total[panel : 2 * panel]
    norm = jnp.sum(norm, axis=1, keepdims=True)
    own = jnp.where(own_flag, 1.0, 0.0)
    other = jnp.where(deflated & (source_half != half), 1.0, 0.0)
    sums_ref[...] = jnp.where(lane == 0, norm, jnp.where(lane == 1, own, jnp.where(lane == 2, other, 0.0)))


def rest_kernel(
    other_ref, split_in, rows_ref, part_ref, sums_ref, shifts_ref, mask_ref, roots_ref,
    out_ref, kept_line, shift_line
):
    other_half = 1 - lax.axis_index("row") // (lax.axis_size("row") // 2)
    panel, first = part_ref.shape
    groups, per_group, _ = out_ref.shape
    height = rows_ref.shape[0]
    width = split_in.shape[1]
    poles(other_half, other_ref[...].astype(jnp.float32), mask_ref, shifts_ref, kept_line, shift_line)
    roots_all = spread(roots_ref[...])
    norm = jnp.zeros((panel, LANES), jnp.float32)
    total = jnp.zeros((2 * panel, height - first), jnp.float32)
    chunk = width // 8
    for c in range(8):
        at = slice(c * chunk, (c + 1) * chunk)
        total = total + lax.dot_general(
            split_in[:, at], rows_ref[first:, at], (((1,), (1,)), ((), ())), preferred_element_type=jnp.float32
        )
        for t in range(c * chunk // LANES, (c + 1) * chunk // LANES):
            cauchy = cauchy_tile(kept_line, shift_line, roots_all, slice(t * LANES, (t + 1) * LANES))
            norm = norm + cauchy * cauchy
    lane = lax.broadcasted_iota(jnp.int32, (panel, LANES), 1)
    extra = sums_ref[...] + jnp.where(lane == 0, jnp.sum(norm, axis=1, keepdims=True), 0.0)
    out_ref[:, :, 0:first] = part_ref[...].reshape(groups, per_group, first)
    out_ref[:, :, first:height] = (total[0:panel] + total[panel : 2 * panel]).reshape(groups, per_group, height - first)
    out_ref[:, :, height:] = extra.reshape(groups, per_group, LANES)


def finish_kernel(parts_ref, out_ref):
    groups = parts_ref.shape[0]
    height = out_ref.shape[1]
    extra = parts_ref[:, :, height:]
    total = jnp.sum(extra, axis=0)
    norm2 = total[:, 0:1]
    deflated = total[:, 1:2] + total[:, 2:3] > 0.5
    scale = 1.0 / jnp.sqrt(norm2)
    result = jnp.zeros(out_ref.shape, jnp.float32)
    for group in range(groups):
        weight = jnp.where(deflated, extra[group, :, 1:2], scale)
        result = result + weight * parts_ref[group, :, 0:height]
    out_ref[...] = jnp.where(deflated & (total[:, 1:2] < 0.5), 0.0, result)


def local(eigvec_rows, split, shifts, roots, deflate_mask, panel_source):
    height, width = eigvec_rows.shape
    row_count = lax.axis_size("row")
    col_count = lax.axis_size("col")
    half_devices = row_count // 2
    panel = roots.shape[0]
    first = height // 2
    lines_shape = (width // PIECE, PIECE)
    vmem = pl.BlockSpec(memory_space=pltpu.VMEM)
    smem = pl.BlockSpec(memory_space=pltpu.SMEM)
    anywhere = pl.BlockSpec(memory_space=pl.ANY)
    limit = lambda mib: pltpu.CompilerParams(vmem_limit_bytes=mib * 2**20)
    struct = jax.ShapeDtypeStruct
    roots = roots.reshape(1, -1)
    panel_source = panel_source.reshape(1, -1)
    lines = pl.pallas_call(
        functools.partial(pick_kernel, height=height),
        out_shape=struct((half_devices, *lines_shape), eigvec_rows.dtype),
        in_specs=[smem, anywhere],
        out_specs=vmem,
        scratch_shapes=[pltpu.VMEM((ALIGN, width), eigvec_rows.dtype), pltpu.SemaphoreType.DMA],
        compiler_params=limit(4),
        name="pick_line",
    )(pltpu.with_memory_space_constraint(split, pltpu.HBM), pltpu.with_memory_space_constraint(eigvec_rows, pltpu.HBM))
    halves = [list(range(half_devices)), list(range(half_devices, row_count))]
    lines = lax.all_to_all(lines, "row", 0, 0, axis_index_groups=halves)
    held = pl.pallas_call(
        functools.partial(held_kernel, height=height),
        out_shape=struct(lines_shape, eigvec_rows.dtype),
        in_specs=[smem, vmem],
        out_specs=vmem,
        compiler_params=limit(4),
        name="held_line",
    )(split, lines)
    flip = half_devices + half_devices // 2
    other = lax.ppermute(held, "row", [(i, i ^ flip) for i in range(row_count)])
    pole_lines = [pltpu.VMEM((1, width), jnp.float32)] * 2
    split_merged, part, sums = pl.pallas_call(
        functools.partial(merge_kernel, height=height, width=width, columns=width * col_count),
        out_shape=(
            struct((2 * panel, width), jnp.bfloat16),
            struct((panel, first), jnp.float32),
            struct((panel, LANES), jnp.float32),
        ),
        in_specs=[smem, vmem, vmem, vmem, vmem, vmem, vmem],
        out_specs=(vmem, vmem, vmem),
        scratch_shapes=[
            pltpu.VMEM((2 * width // LANES, LANES), jnp.float32),
            *pole_lines,
        ],
        compiler_params=limit(12),
        cost_estimate=pl.CostEstimate(flops=10**9, bytes_accessed=2**24, transcendentals=2**20),
        name="merge_columns",
    )(split, lines, eigvec_rows, shifts, deflate_mask, roots, panel_source)
    parts = pl.pallas_call(
        rest_kernel,
        out_shape=struct((col_count, panel // col_count, height + LANES), jnp.float32),
        in_specs=[vmem] * 8,
        out_specs=vmem,
        scratch_shapes=pole_lines,
        compiler_params=limit(12),
        cost_estimate=pl.CostEstimate(flops=10**9, bytes_accessed=2**23, transcendentals=2**20),
        name="rest_product",
    )(other, split_merged, eigvec_rows, part, sums, shifts, deflate_mask, roots)
    parts = lax.all_to_all(parts, "col", 0, 0)
    return pl.pallas_call(
        finish_kernel,
        out_shape=struct((panel // col_count, height), jnp.float32),
        in_specs=[vmem],
        out_specs=vmem,
        compiler_params=limit(4),
        name="scale_and_add",
    )(parts)


def solution(mesh):
    return jax.shard_map(
        local,
        mesh=mesh,
        in_specs=(P("row", "col"), P(), P(None, "col"), P(), P(None, "col"), P()),
        out_specs=P("col", "row"),
        check_vma=False,
    )
```

time: 53.4 us -> 46.9 us (0.88)
  waiting for transfers between devices: 3.45 us -> 0.01 us
  local copies, waits for them, and re-layouts: 3.4 us -> 0.02 us
    ppermute x1, waiting for transfers between devices: 3.45 us -> 0.01 us  [local(): other = lax.ppermute(held, 'row', [(i, i ^ flip) for i in range(row_count)])]
    unnamed x12, local copies, waits for them, and re-layouts: 3.4 us -> 0.02 us
    pallas_call x1, Pallas kernels: 3.78 us -> 5.02 us  [local(): pl.pallas_call(functools.partial(merge_kernel, height=height, width=width...]
    pallas_call x3 -> x4, Pallas kernels: 6.71 us -> 5.86 us  [the longest x1 2.29 us: local(): pl.pallas_call(rest_kernel, out_shape=struct((col_count, panel // col_cou...]
  transfers between devices with their start and end apart: 1 -> 1, of which waited for: 1 -> 0; matrix products, arithmetic and copies ran while one was open for 0% -> 0% of each run, Pallas kernels for 0% -> 11%
where the time goes in v2:
time: 46.9 us; the launch traced here: 46.7 us
  blocking collectives  33.1 us (71%)
  Pallas kernels  10.9 us (23%)
  starting transfers between devices  2.61 us (6%)
    all_to_all x1, blocking collectives, local(): parts = lax.all_to_all(parts, 'col', 0, 0)  21.9 us
    all_to_all x1, blocking collectives, local(): lines = lax.all_to_all(lines, 'row', 0, 0, axis_index_groups=halves)  11.2 us
    pallas_call x1, Pallas kernels, local(): pl.pallas_call(functools.partial(merge_kernel, height=height, width=width...  5.02 us
    ppermute x1, starting transfers between devices, local(): other = lax.ppermute(held, 'row', [(i, i ^ flip) for i in range(row_count)])  2.61 us
    pallas_call x1, Pallas kernels, local(): pl.pallas_call(rest_kernel, out_shape=struct((col_count, panel // col_cou...  2.29 us
    pallas_call x1, Pallas kernels, local(): pl.pallas_call(functools.partial(pick_kernel, height=height), out_shape=s...  2.21 us
  transfers between devices with their start and end apart: 1, of which 0 were waited for; matrix products, arithmetic and copies ran while one was open for 0% of the time, Pallas kernels for 11%

profile of v2, /device:TPU:8, one launch (start us, length us, event | category | flops | bytes accessed | tf_op | source)
XLA Modules:
  0.0 46.7 jit_solution(13537043785592484810)
XLA Ops:
  0.0 0.0 copy-start.3
  0.0 0.0 copy-start
  0.0 0.0 copy-start.2
  0.0 0.0 copy-start.1
  0.0 0.0 copy-start.5
  0.0 0.0 copy-start.4
  0.0 2.2 %pick_line.1 = bf16[16,16,512]{2,1,0:T(8,128)(2,1)S(1)} custom-call(s32[2]{0:T(128)} %split_ref.5, bf16[512,8192]{1,0:T(8,128)(2,1)} %rows_ref.5), custom_call_target="tpu_custom_call" | custom-call | tf_op jit(solution)/shard_map/pick_line/pallas_call | solution.py:178
  2.3 11.2 %all_to_all.10.lines_ref = bf16[16,16,512]{2,1,0:T(8,128)(2,1)S(1)} all-to-all(bf16[16,16,512]{2,1,0:T(8,128)(2,1)S(1)} %pick_line.1), channel_id=1, replica_groups={{0,8,16,24,32,40,48,56,64,72,80,88,96,104,112,120},{128,136,144,152,160..., dimensions={0} | all-to-all | bytes 524288 | tf_op jit(solution)/shard_map/all_to_all | solution.py:188
  13.5 0.0 copy-done.3
  13.5 0.6 %held_line.1 = bf16[16,512]{1,0:T(8,128)(2,1)S(1)} custom-call(s32[2]{0:T(128)S(1)} %copy-done.3, bf16[16,16,512]{2,1,0:T(8,128)(2,1)S(1)} %all_to_all.10.lines_ref), custom_call_target="tpu_custom_call" | custom-call | tf_op jit(solution)/shard_map/held_line/pallas_call | solution.py:189
  14.1 2.6 %collective-permute-start = (bf16[16,512]{1,0:T(8,128)(2,1)S(1)}, bf16[16,512]{1,0:T(8,128)(2,1)S(1)}, u32[]{:S(2)}, u32[]{:S(2)}) collective-permute-start(bf16[16,512]{1,0:T(8,128)(2,1)S(1)} %held_line.1), channel_id=1, source_target_pairs={{0,192},{8,200},{16,208},{24,216},{32,224},{40,232},{48,240},{56,2... | collective-permute-start | bytes 49160 | tf_op jit(solution)/shard_map/ppermute | solution.py:198
  16.7 0.0 copy-done
  16.7 0.0 copy-done.2
  16.7 0.0 copy-done.1
  16.7 0.0 copy-done.5
  16.7 0.0 copy-done.4
  16.7 5.0 %merge_columns.1 = (bf16[256,8192]{1,0:T(8,128)(2,1)S(1)}, f32[128,256]{1,0:T(8,128)S(1)}, f32[128,128]{1,0:T(8,128)S(1)}) custom-call(s32[2]{0:T(128)S(1)} %copy-done.3, bf16[16,16,512]{2,1,0:T(8,128)(2,1)S(1)} %all_to_all.10.lines_ref, bf16[512,8192]{1,0:T(8,128)(2,1)S(1)} %copy-done, f32[2,8192]{1,0:T(2,128)S(1)} %copy-done.1, s32[2,8192]{1,0:T(2,128)S(1)} %copy-done.2, ...), custom_call_target="tpu_custom_call" | custom-call | flops 1000000000 | bytes 16777216 | tf_op jit(solution)/shard_map/merge_columns/pallas_call | solution.py:200
  21.7 0.0 collective-permute-done.other_ref
  21.7 2.3 %rest_product.1 = f32[8,16,640]{2,1,0:T(8,128)S(1)} custom-call(bf16[16,512]{1,0:T(8,128)(2,1)S(1)} %collective-permute-done.other_ref, bf16[256,8192]{1,0:T(8,128)(2,1)S(1)} %get-tuple-element.8.split_in, bf16[512,8192]{1,0:T(8,128)(2,1)S(1)} %copy-done, f32[128,256]{1,0:T(8,128)S(1)} %get-tuple-element.9.part_ref, ...), custom_call_target="tpu_custom_call" | custom-call | flops 1000000000 | bytes 8388608 | tf_op jit(solution)/shard_map/rest_product/pallas_call | solution.py:217
  24.0 21.9 %all_to_all.11.parts_ref = f32[8,16,640]{2,1,0:T(8,128)S(1)} all-to-all(f32[8,16,640]{2,1,0:T(8,128)S(1)} %rest_product.1), channel_id=1, replica_groups=mesh['row'=32,'col'=8] {'col'}, dimensions={0} | all-to-all | bytes 655360 | tf_op jit(solution)/shard_map/all_to_all | solution.py:227
  45.9 0.8 %scale_and_add.1 = f32[16,512]{1,0:T(8,128)} custom-call(f32[8,16,640]{2,1,0:T(8,128)S(1)} %all_to_all.11.parts_ref), custom_call_target="tpu_custom_call" | custom-call | tf_op jit(solution)/shard_map/scale_and_add/pallas_call | solution.py:228
Async XLA Ops:
  0.0 13.5 %copy-start.3 = (s32[2]{0:T(128)S(1)}, s32[2]{0:T(128)}, u32[]{:S(2)}) copy-start(s32[2]{0:T(128)} %split_ref.5) | copy-start | bytes 28
  0.0 16.7 %copy-start = (bf16[512,8192]{1,0:T(8,128)(2,1)S(1)}, bf16[512,8192]{1,0:T(8,128)(2,1)}, u32[]{:S(2)}) copy-start(bf16[512,8192]{1,0:T(8,128)(2,1)} %rows_ref.5) | copy-start | bytes 25165828
  0.0 16.7 %copy-start.2 = (s32[2,8192]{1,0:T(2,128)S(1)}, s32[2,8192]{1,0:T(2,128)}, u32[]{:S(2)}) copy-start(s32[2,8192]{1,0:T(2,128)} %mask_ref.3) | copy-start | bytes 196612
  0.0 16.7 %copy-start.1 = (f32[2,8192]{1,0:T(2,128)S(1)}, f32[2,8192]{1,0:T(2,128)}, u32[]{:S(2)}) copy-start(f32[2,8192]{1,0:T(2,128)} %shifts_ref.3) | copy-start | bytes 196612
  0.0 16.7 %copy-start.5 = (s32[128]{0:T(128)S(1)}, s32[128]{0:T(128)}, u32[]{:S(2)}) copy-start(s32[128]{0:T(128)} %param.11) | copy-start | bytes 1540
  0.0 16.7 %copy-start.4 = (f32[128]{0:T(128)S(1)}, f32[128]{0:T(128)}, u32[]{:S(2)}) copy-start(f32[128]{0:T(128)} %param.9) | copy-start | bytes 1540
  14.1 7.7 %collective-permute-start = (bf16[16,512]{1,0:T(8,128)(2,1)S(1)}, bf16[16,512]{1,0:T(8,128)(2,1)S(1)}, u32[]{:S(2)}, u32[]{:S(2)}) collective-permute-start(bf16[16,512]{1,0:T(8,128)(2,1)S(1)} %held_line.1), channel_id=1, source_target_pairs={{0,192},{8,200},{16,208},{24,216},{32,224},{40,232},{48,240},{56,2... | collective-permute-start | bytes 49160 | tf_op jit(solution)/shard_map/ppermute | solution.py:198

commit v3 on v2

v3 whole, which is shorter than its diff:
```python
import functools

import jax
import jax.numpy as jnp
from jax import lax
from jax.experimental import pallas as pl
from jax.experimental.pallas import tpu as pltpu
from jax.sharding import PartitionSpec as P

LANES = 128
ALIGN = 16
SUBLANES = 8
CHUNKS = 8


def pick_kernel(split_ref, rows_ref, out_ref, window, sem, *, height):
    half = lax.axis_index("row") // (lax.axis_size("row") // 2)
    row = split_ref[half] % height
    base = pl.multiple_of((row // ALIGN) * ALIGN, ALIGN)
    copy = pltpu.make_async_copy(rows_ref.at[pl.ds(base, ALIGN)], window, sem)
    copy.start()
    copy.wait()
    inner = row - base
    lower = inner < SUBLANES
    inner = lax.rem(inner, SUBLANES)
    sublane = lax.broadcasted_iota(jnp.int32, (SUBLANES, LANES), 0)
    blocks = [jnp.zeros((SUBLANES, LANES), jnp.float32) for _ in range(out_ref.shape[1] // SUBLANES)]
    for a in range(out_ref.shape[1]):
        both = window[:, a * LANES : (a + 1) * LANES].astype(jnp.float32)
        eight = jnp.where(lower, both[0:SUBLANES], both[SUBLANES:])
        target = a % SUBLANES
        turned = pltpu.roll(eight, lax.rem(target - inner + SUBLANES, SUBLANES), 0)
        blocks[a // SUBLANES] = jnp.where(sublane == target, turned, blocks[a // SUBLANES])
    line = jnp.concatenate(blocks, axis=0).astype(out_ref.dtype)
    for target in range(out_ref.shape[0]):
        out_ref[target] = line


def held_kernel(split_ref, lines_ref, out_ref, *, height):
    half = lax.axis_index("row") // (lax.axis_size("row") // 2)
    out_ref[...] = lines_ref[split_ref[half] // height]


def spread(line):
    return jnp.broadcast_to(line, (LANES, line.shape[1])).T


def merge_kernel(
    line_ref, _, shifts_ref, mask_ref, roots_ref, source_ref,
    split_out, sums_ref, kept_line, shift_line, *, columns
):
    half = lax.axis_index("row") // (lax.axis_size("row") // 2)
    col = lax.axis_index("col")
    panel = roots_ref.shape[1]
    tiles = line_ref.shape[0]
    width = tiles * LANES
    source = spread(source_ref[...])
    source_half = (source >= columns).astype(jnp.int32)
    local = source - source_half * columns - col * width
    here = (local >= 0) & (local < width)
    lane = lax.broadcasted_iota(jnp.int32, (panel, LANES), 1)
    tile_of = jnp.where(here, local // LANES * 2 + source_half, -1)
    picked = jnp.dot(
        jnp.where(lax.broadcasted_iota(jnp.int32, (panel, 2 * tiles), 1) == tile_of[:, 0:1], 1.0, 0.0).astype(jnp.bfloat16),
        mask_ref[...].astype(jnp.float32).astype(jnp.bfloat16),
        preferred_element_type=jnp.float32,
    )
    deflated = jnp.sum(jnp.where(lane == local % LANES, picked, 0.0), axis=1, keepdims=True) > 0.5
    own_flag = deflated & (source_half == half)
    roots_all = jnp.where(own_flag, 3e38, spread(roots_ref[...]))
    unit_all = jnp.where(own_flag, local, -1)
    first_lane = lax.broadcasted_iota(jnp.int32, (1, LANES), 1)
    kept_line[...] = jnp.where(mask_ref[pl.ds(half, tiles, stride=2), :] == 1, 0.0, line_ref[...].astype(jnp.float32))
    shift_line[...] = shifts_ref[pl.ds(half, tiles, stride=2), :]

    def fill(t, norm):
        at = pl.ds(pl.multiple_of(t * LANES, LANES), LANES)
        cauchy = kept_line[pl.ds(t, 1), :] * pltpu.reciprocal(shift_line[pl.ds(t, 1), :] - roots_all, approx=True)
        value = jnp.where(unit_all == first_lane + t * LANES, 1.0, cauchy)
        high = value.astype(jnp.bfloat16)
        split_out[0:panel, at] = high
        split_out[panel : 2 * panel, at] = (value - high.astype(jnp.float32)).astype(jnp.bfloat16)
        return norm + cauchy * cauchy

    norm = lax.fori_loop(0, tiles, fill, jnp.zeros((panel, LANES), jnp.float32), unroll=1)
    norm = jnp.sum(norm, axis=1, keepdims=True)
    own = jnp.where(own_flag, 1.0, 0.0)
    other = jnp.where(deflated & (source_half != half), 1.0, 0.0)
    sums_ref[...] = jnp.where(lane == 0, norm, jnp.where(lane == 1, own, jnp.where(lane == 2, other, 0.0)))


def product_kernel(
    other_ref, split_in, rows_ref, sums_ref, shifts_ref, mask_ref, roots_ref, out_ref, kept_line, shift_line
):
    other_half = 1 - lax.axis_index("row") // (lax.axis_size("row") // 2)
    panel = roots_ref.shape[1]
    groups, per_group, _ = out_ref.shape
    height, width = rows_ref.shape
    tiles = width // LANES
    kept_line[...] = jnp.where(
        mask_ref[pl.ds(other_half, tiles, stride=2), :] == 1, 0.0, other_ref[...].astype(jnp.float32)
    )
    shift_line[...] = shifts_ref[pl.ds(other_half, tiles, stride=2), :]
    roots_all = spread(roots_ref[...])
    norm = jnp.zeros((panel, LANES), jnp.float32)
    total = jnp.zeros((2 * panel, height), jnp.float32)
    chunk = width // CHUNKS
    for c in range(CHUNKS):
        at = slice(c * chunk, (c + 1) * chunk)
        total = total + lax.dot_general(
            split_in[:, at], rows_ref[:, at], (((1,), (1,)), ((), ())), preferred_element_type=jnp.float32
        )
        for t in range(c * chunk // LANES, (c + 1) * chunk // LANES):
            cauchy = kept_line[t : t + 1, :] * pltpu.reciprocal(shift_line[t : t + 1, :] - roots_all, approx=True)
            norm = norm + cauchy * cauchy
    lane = lax.broadcasted_iota(jnp.int32, (panel, LANES), 1)
    extra = sums_ref[...] + jnp.where(lane == 0, jnp.sum(norm, axis=1, keepdims=True), 0.0)
    out_ref[:, :, 0:height] = (total[0:panel] + total[panel : 2 * panel]).reshape(groups, per_group, height)
    out_ref[:, :, height:] = extra.reshape(groups, per_group, LANES)


def finish_kernel(parts_ref, out_ref):
    groups = parts_ref.shape[0]
    height = out_ref.shape[1]
    extra = parts_ref[:, :, height:]
    total = jnp.sum(extra, axis=0)
    norm2 = total[:, 0:1]
    deflated = total[:, 1:2] + total[:, 2:3] > 0.5
    scale = 1.0 / jnp.sqrt(norm2)
    result = jnp.zeros(out_ref.shape, jnp.float32)
    for group in range(groups):
        weight = jnp.where(deflated, extra[group, :, 1:2], scale)
        result = result + weight * parts_ref[group, :, 0:height]
    out_ref[...] = jnp.where(deflated & (total[:, 1:2] < 0.5), 0.0, result)


def local(eigvec_rows, split, shifts, roots, deflate_mask, panel_source):
    height, width = eigvec_rows.shape
    row_count = lax.axis_size("row")
    col_count = lax.axis_size("col")
    half_devices = row_count // 2
    panel = roots.shape[0]
    tiles = width // LANES
    vmem = pl.BlockSpec(memory_space=pltpu.VMEM)
    smem = pl.BlockSpec(memory_space=pltpu.SMEM)
    anywhere = pl.BlockSpec(memory_space=pl.ANY)
    limit = lambda mib: pltpu.CompilerParams(vmem_limit_bytes=mib * 2**20)
    in_hbm = lambda x: pltpu.with_memory_space_constraint(x, pltpu.HBM)
    square = lambda x: x.reshape(2, tiles, LANES).swapaxes(0, 1).reshape(2 * tiles, LANES)
    struct = jax.ShapeDtypeStruct
    roots = roots.reshape(1, -1)
    panel_source = panel_source.reshape(1, -1)
    shifts = square(shifts)
    deflate_mask = square(deflate_mask)
    lines = pl.pallas_call(
        functools.partial(pick_kernel, height=height),
        out_shape=struct((half_devices, tiles, LANES), eigvec_rows.dtype),
        in_specs=[smem, anywhere],
        out_specs=vmem,
        scratch_shapes=[pltpu.VMEM((ALIGN, width), eigvec_rows.dtype), pltpu.SemaphoreType.DMA],
        compiler_params=limit(4),
        name="pick_line",
    )(in_hbm(split), in_hbm(eigvec_rows))
    halves = [list(range(half_devices)), list(range(half_devices, row_count))]
    lines = lax.all_to_all(lines, "row", 0, 0, axis_index_groups=halves)
    line = pl.pallas_call(
        functools.partial(held_kernel, height=height),
        out_shape=struct((tiles, LANES), eigvec_rows.dtype),
        in_specs=[smem, vmem],
        out_specs=vmem,
        compiler_params=limit(4),
        name="held_line",
    )(split, lines)
    flip = half_devices + half_devices // 2
    other = lax.ppermute(line, "row", [(i, i ^ flip) for i in range(row_count)])
    pole_lines = [pltpu.VMEM((tiles, LANES), jnp.float32)] * 2
    split_merged, sums = pl.pallas_call(
        functools.partial(merge_kernel, columns=width * col_count),
        out_shape=(
            struct((2 * panel, width), jnp.bfloat16),
            struct((panel, LANES), jnp.float32),
        ),
        in_specs=[vmem] * 6,
        out_specs=(vmem, vmem),
        scratch_shapes=pole_lines,
        compiler_params=limit(8),
        cost_estimate=pl.CostEstimate(flops=10**9, bytes_accessed=2**24, transcendentals=2**20),
        name="merge_columns",
    )(line, eigvec_rows, shifts, deflate_mask, roots, panel_source)
    parts = pl.pallas_call(
        product_kernel,
        out_shape=struct((col_count, panel // col_count, height + LANES), jnp.float32),
        in_specs=[vmem] * 7,
        out_specs=vmem,
        scratch_shapes=pole_lines,
        compiler_params=limit(12),
        cost_estimate=pl.CostEstimate(flops=2 * 10**9, bytes_accessed=2**23, transcendentals=2**20),
        name="block_product",
    )(other, split_merged, eigvec_rows, sums, shifts, deflate_mask, roots)
    parts = lax.all_to_all(parts, "col", 0, 0)
    return pl.pallas_call(
        finish_kernel,
        out_shape=struct((panel // col_count, height), jnp.float32),
        in_specs=[vmem],
        out_specs=vmem,
        compiler_params=limit(4),
        name="scale_and_add",
    )(parts)


def solution(mesh):
    return jax.shard_map(
        local,
        mesh=mesh,
        in_specs=(P("row", "col"), P(), P(None, "col"), P(), P(None, "col"), P()),
        out_specs=P("col", "row"),
        check_vma=False,
    )
```

time: 46.9 us -> 45.5 us (0.970)
  Pallas kernels: 10.9 us -> 9.44 us
    pallas_call x2, Pallas kernels: 7.31 us -> 5.88 us  [the longest x1 2.97 us: local(): pl.pallas_call(functools.partial(merge_kernel, columns=width * col_count)...]
  transfers between devices with their start and end apart: 1 -> 1, of which waited for: 0 -> 0; matrix products, arithmetic and copies ran while one was open for 0% -> 0% of each run, Pallas kernels for 11% -> 7%
where the time goes in v3:
time: 45.5 us; the launch traced here: 45.3 us
  blocking collectives  33.1 us (73%)
  Pallas kernels  9.44 us (21%)
  starting transfers between devices  2.61 us (6%)
    all_to_all x1, blocking collectives, local(): parts = lax.all_to_all(parts, 'col', 0, 0)  21.9 us
    all_to_all x1, blocking collectives, local(): lines = lax.all_to_all(lines, 'row', 0, 0, axis_index_groups=halves)  11.2 us
    pallas_call x1, Pallas kernels, local(): pl.pallas_call(functools.partial(merge_kernel, columns=width * col_count)...  2.97 us
    pallas_call x1, Pallas kernels, local(): pl.pallas_call(product_kernel, out_shape=struct((col_count, panel // col_...  2.91 us
    ppermute x1, starting transfers between devices, local(): other = lax.ppermute(line, 'row', [(i, i ^ flip) for i in range(row_count)])  2.61 us
    pallas_call x1, Pallas kernels, local(): pl.pallas_call(functools.partial(pick_kernel, height=height), out_shape=s...  2.21 us
  transfers between devices with their start and end apart: 1, of which 0 were waited for; matrix products, arithmetic and copies ran while one was open for 0% of the time, Pallas kernels for 7%

profile of v3, /device:TPU:8, one launch (start us, length us, event | category | flops | bytes accessed | tf_op | source)
XLA Modules:
  0.0 45.3 jit_solution(10345513439952625482)
XLA Ops:
  0.0 0.0 copy-start
  0.0 0.0 copy-start.3
  0.0 0.0 copy-start.5
  0.0 0.0 copy-start.2
  0.0 0.0 copy-start.4
  0.0 0.0 copy-start.1
  0.0 2.2 %pick_line.1 = bf16[16,64,128]{2,1,0:T(8,128)(2,1)S(1)} custom-call(s32[2]{0:T(128)} %split_ref.3, bf16[512,8192]{1,0:T(8,128)(2,1)} %rows_ref.3), custom_call_target="tpu_custom_call" | custom-call | tf_op jit(solution)/shard_map/pick_line/pallas_call | solution.py:155
  2.3 11.2 %all_to_all.10.lines_ref = bf16[16,64,128]{2,1,0:T(8,128)(2,1)S(1)} all-to-all(bf16[16,64,128]{2,1,0:T(8,128)(2,1)S(1)} %pick_line.1), channel_id=1, replica_groups={{0,8,16,24,32,40,48,56,64,72,80,88,96,104,112,120},{128,136,144,152,160..., dimensions={0} | all-to-all | bytes 524288 | tf_op jit(solution)/shard_map/all_to_all | solution.py:165
  13.5 0.0 copy-done.3
  13.5 0.6 %held_line.1.line_ref = bf16[64,128]{1,0:T(8,128)(2,1)S(1)} custom-call(s32[2]{0:T(128)S(1)} %copy-done.3, bf16[16,64,128]{2,1,0:T(8,128)(2,1)S(1)} %all_to_all.10.lines_ref), custom_call_target="tpu_custom_call" | custom-call | tf_op jit(solution)/shard_map/held_line/pallas_call | solution.py:166
  14.1 2.6 %collective-permute-start = (bf16[64,128]{1,0:T(8,128)(2,1)S(1)}, bf16[64,128]{1,0:T(8,128)(2,1)S(1)}, u32[]{:S(2)}, u32[]{:S(2)}) collective-permute-start(bf16[64,128]{1,0:T(8,128)(2,1)S(1)} %held_line.1.line_ref), channel_id=1, source_target_pairs={{0,192},{8,200},{16,208},{24,216},{32,224},{40,232},{48,240},{56,2... | collective-permute-start | bytes 49160 | tf_op jit(solution)/shard_map/ppermute | solution.py:175
  16.7 0.0 copy-done
  16.7 0.0 copy-done.5
  16.7 0.0 copy-done.2
  16.7 0.0 copy-done.4
  16.7 0.0 copy-done.1
  16.7 3.0 %merge_columns.1 = (bf16[256,8192]{1,0:T(8,128)(2,1)S(1)}, f32[128,128]{1,0:T(8,128)S(1)}) custom-call(bf16[64,128]{1,0:T(8,128)(2,1)S(1)} %held_line.1.line_ref, bf16[512,8192]{1,0:T(8,128)(2,1)S(1)} %copy-done, f32[128,128]{1,0:T(8,128)S(1)} %bitcast.12, s32[128,128]{1,0:T(8,128)S(1)} %bitcast.14, f32[1,128]{1,0:T(1,128)S(1)} %bitcast.16, ...), custom_call_target="tpu_custom_call" | custom-call | flops 1000000000 | bytes 16777216 | tf_op jit(solution)/shard_map/merge_columns/pallas_call | solution.py:177
  19.7 0.0 collective-permute-done.other_ref
  19.7 2.9 %block_product.1 = f32[8,16,640]{2,1,0:T(8,128)S(1)} custom-call(bf16[64,128]{1,0:T(8,128)(2,1)S(1)} %collective-permute-done.other_ref, bf16[256,8192]{1,0:T(8,128)(2,1)S(1)} %get-tuple-element.7.split_in, bf16[512,8192]{1,0:T(8,128)(2,1)S(1)} %copy-done, f32[128,128]{1,0:T(8,128)S(1)} %get-tuple-element.8.sums_ref, f32[128,128]{1,0:T(8,128)S(1)} %bitcast.13, ...), custom_call_target="tpu_custom_call" | custom-call | flops 2000000000 | bytes 8388608 | tf_op jit(solution)/shard_map/block_product/pallas_call | solution.py:190
  22.6 21.9 %all_to_all.11.parts_ref = f32[8,16,640]{2,1,0:T(8,128)S(1)} all-to-all(f32[8,16,640]{2,1,0:T(8,128)S(1)} %block_product.1), channel_id=1, replica_groups=mesh['row'=32,'col'=8] {'col'}, dimensions={0} | all-to-all | bytes 655360 | tf_op jit(solution)/shard_map/all_to_all | solution.py:200
  44.5 0.8 %scale_and_add.1 = f32[16,512]{1,0:T(8,128)} custom-call(f32[8,16,640]{2,1,0:T(8,128)S(1)} %all_to_all.11.parts_ref), custom_call_target="tpu_custom_call" | custom-call | tf_op jit(solution)/shard_map/scale_and_add/pallas_call | solution.py:201
Async XLA Ops:
  0.0 16.7 %copy-start = (bf16[512,8192]{1,0:T(8,128)(2,1)S(1)}, bf16[512,8192]{1,0:T(8,128)(2,1)}, u32[]{:S(2)}) copy-start(bf16[512,8192]{1,0:T(8,128)(2,1)} %rows_ref.3) | copy-start | bytes 25165828
  0.0 13.5 %copy-start.3 = (s32[2]{0:T(128)S(1)}, s32[2]{0:T(128)}, u32[]{:S(2)}) copy-start(s32[2]{0:T(128)} %split_ref.3) | copy-start | bytes 28
  0.0 16.7 %copy-start.5 = (s32[128]{0:T(128)S(1)}, s32[128]{0:T(128)}, u32[]{:S(2)}) copy-start(s32[128]{0:T(128)} %param.11) | copy-start | bytes 1540
  0.0 16.7 %copy-start.2 = (s32[2,8192]{1,0:T(2,128)S(1)}, s32[2,8192]{1,0:T(2,128)}, u32[]{:S(2)}) copy-start(s32[2,8192]{1,0:T(2,128)} %param.10) | copy-start | bytes 196612
  0.0 16.7 %copy-start.4 = (f32[128]{0:T(128)S(1)}, f32[128]{0:T(128)}, u32[]{:S(2)}) copy-start(f32[128]{0:T(128)} %param.9) | copy-start | bytes 1540
  0.0 16.7 %copy-start.1 = (f32[2,8192]{1,0:T(2,128)S(1)}, f32[2,8192]{1,0:T(2,128)}, u32[]{:S(2)}) copy-start(f32[2,8192]{1,0:T(2,128)} %param.8) | copy-start | bytes 196612
  14.1 5.6 %collective-permute-start = (bf16[64,128]{1,0:T(8,128)(2,1)S(1)}, bf16[64,128]{1,0:T(8,128)(2,1)S(1)}, u32[]{:S(2)}, u32[]{:S(2)}) collective-permute-start(bf16[64,128]{1,0:T(8,128)(2,1)S(1)} %held_line.1.line_ref), channel_id=1, source_target_pairs={{0,192},{8,200},{16,208},{24,216},{32,224},{40,232},{48,240},{56,2... | collective-permute-start | bytes 49160 | tf_op jit(solution)/shard_map/ppermute | solution.py:175

commit v4 on v3

v4 whole, which is shorter than its diff:
```python
import functools

import jax
import jax.numpy as jnp
from jax import lax
from jax.experimental import pallas as pl
from jax.experimental.pallas import tpu as pltpu
from jax.sharding import PartitionSpec as P

LANES = 128
ALIGN = 16
SUBLANES = 8
CHUNKS = 8


def pick_kernel(split_ref, rows_ref, out_ref, window, sem, *, height):
    half = lax.axis_index("row") // (lax.axis_size("row") // 2)
    row = split_ref[half] % height
    base = pl.multiple_of((row // ALIGN) * ALIGN, ALIGN)
    copy = pltpu.make_async_copy(rows_ref.at[pl.ds(base, ALIGN)], window, sem)
    copy.start()
    copy.wait()
    inner = row - base
    lower = inner < SUBLANES
    inner = lax.rem(inner, SUBLANES)
    sublane = lax.broadcasted_iota(jnp.int32, (SUBLANES, LANES), 0)
    blocks = [jnp.zeros((SUBLANES, LANES), jnp.float32) for _ in range(out_ref.shape[1] // SUBLANES)]
    for a in range(out_ref.shape[1]):
        both = window[:, a * LANES : (a + 1) * LANES].astype(jnp.float32)
        eight = jnp.where(lower, both[0:SUBLANES], both[SUBLANES:])
        target = a % SUBLANES
        turned = pltpu.roll(eight, lax.rem(target - inner + SUBLANES, SUBLANES), 0)
        blocks[a // SUBLANES] = jnp.where(sublane == target, turned, blocks[a // SUBLANES])
    line = jnp.concatenate(blocks, axis=0).astype(out_ref.dtype)
    for target in range(out_ref.shape[0]):
        out_ref[target] = line


def spread(line):
    return jnp.broadcast_to(line, (LANES, line.shape[1])).T


def norm_kernel(
    split_ref, lines_ref, _, shifts_ref, mask_ref, roots_ref, source_ref,
    norm_ref, sums_ref, kept_ref, own_shifts_ref, poles_ref, unit_ref, *, height, columns
):
    half = lax.axis_index("row") // (lax.axis_size("row") // 2)
    col = lax.axis_index("col")
    panel = roots_ref.shape[1]
    tiles = lines_ref.shape[1]
    width = tiles * LANES
    line = lines_ref[split_ref[half] // height].astype(jnp.float32)
    kept_ref[...] = jnp.where(mask_ref[pl.ds(half, tiles, stride=2), :] == 1, 0.0, line)
    own_shifts_ref[...] = shifts_ref[pl.ds(half, tiles, stride=2), :]
    roots_all = spread(roots_ref[...])
    source = spread(source_ref[...])
    source_half = (source >= columns).astype(jnp.int32)
    local = source - source_half * columns - col * width
    here = (local >= 0) & (local < width)
    lane = lax.broadcasted_iota(jnp.int32, (panel, LANES), 1)
    tile_of = jnp.where(here, local // LANES * 2 + source_half, -1)
    picked = jnp.dot(
        jnp.where(lax.broadcasted_iota(jnp.int32, (panel, 2 * tiles), 1) == tile_of[:, 0:1], 1.0, 0.0).astype(jnp.bfloat16),
        mask_ref[...].astype(jnp.float32).astype(jnp.bfloat16),
        preferred_element_type=jnp.float32,
    )
    deflated = jnp.sum(jnp.where(lane == local % LANES, picked, 0.0), axis=1, keepdims=True) > 0.5
    own_flag = deflated & (source_half == half)
    poles_ref[...] = jnp.where(own_flag, 3e38, roots_all)
    unit_ref[...] = jnp.where(own_flag, local, -1)
    norm = jnp.zeros((panel, LANES), jnp.float32)
    for t in range(tiles):
        cauchy = kept_ref[t : t + 1, :] * pltpu.reciprocal(own_shifts_ref[t : t + 1, :] - roots_all, approx=True)
        norm = norm + cauchy * cauchy
    norm = jnp.sum(norm, axis=1, keepdims=True)
    own = jnp.where(own_flag, 1.0, 0.0)
    other = jnp.where(deflated & (source_half != half), 1.0, 0.0)
    sums = jnp.where(lane == 0, norm, jnp.where(lane == 1, own, jnp.where(lane == 2, other, 0.0))).T[0:SUBLANES]
    norm_ref[...] = jnp.where(lax.broadcasted_iota(jnp.int32, (SUBLANES, LANES), 0) == 0, sums, 0.0)
    sums_ref[...] = sums


def product_kernel(kept_ref, shifts_ref, poles_ref, unit_ref, rows_ref, out_ref):
    panel = poles_ref.shape[0]
    groups = out_ref.shape[0]
    per_group = panel // groups
    height, width = rows_ref.shape
    poles = poles_ref[...]
    unit = unit_ref[...]
    lane = lax.broadcasted_iota(jnp.int32, (1, LANES), 1)
    total = jnp.zeros((2 * panel, height), jnp.float32)
    chunk = width // CHUNKS
    for c in range(CHUNKS):
        highs, lows = [], []
        for t in range(c * chunk // LANES, (c + 1) * chunk // LANES):
            cauchy = kept_ref[t : t + 1, :] * pltpu.reciprocal(shifts_ref[t : t + 1, :] - poles, approx=True)
            value = jnp.where(unit == lane + t * LANES, 1.0, cauchy)
            high = value.astype(jnp.bfloat16)
            highs.append(high)
            lows.append((value - high.astype(jnp.float32)).astype(jnp.bfloat16))
        merged = jnp.concatenate([jnp.concatenate(highs, axis=1), jnp.concatenate(lows, axis=1)], axis=0)
        total = total + lax.dot_general(
            merged, rows_ref[:, c * chunk : (c + 1) * chunk], (((1,), (1,)), ((), ())),
            preferred_element_type=jnp.float32,
        )
    product = (total[0:panel] + total[panel : 2 * panel]).reshape(groups, per_group, height)
    for q in range(height // LANES):
        out_ref[:, q * per_group : (q + 1) * per_group, :] = product[:, :, q * LANES : (q + 1) * LANES]
    out_ref[:, per_group * height // LANES :, :] = jnp.zeros((groups, SUBLANES, LANES), jnp.float32)


def finish_kernel(parts_ref, out_ref, columns_ref):
    groups = parts_ref.shape[0]
    per_group, height = out_ref.shape
    body = per_group * height // LANES
    columns_ref[...] = parts_ref[:, body:, :].reshape(groups * SUBLANES, LANES).T
    start = pl.multiple_of(lax.axis_index("col") * per_group, per_group)
    sums = columns_ref[pl.ds(start, per_group), :]
    kind = lax.broadcasted_iota(jnp.int32, sums.shape, 1) % SUBLANES
    norm2, own, other = (jnp.sum(jnp.where(kind == k, sums, 0.0), axis=1, keepdims=True) for k in range(3))
    scale = 1.0 / jnp.sqrt(norm2)
    blocks = [jnp.zeros((per_group, LANES), jnp.float32) for _ in range(height // LANES)]
    for group in range(groups):
        flag = sums[:, group * SUBLANES + 1 : group * SUBLANES + 2]
        weight = jnp.where(own + other > 0.5, flag, scale)
        for q in range(height // LANES):
            blocks[q] = blocks[q] + weight * parts_ref[group, q * per_group : (q + 1) * per_group, :]
    for q in range(height // LANES):
        out_ref[:, q * LANES : (q + 1) * LANES] = jnp.where(other > 0.5, 0.0, blocks[q])


def local(eigvec_rows, split, shifts, roots, deflate_mask, panel_source):
    height, width = eigvec_rows.shape
    row_count = lax.axis_size("row")
    col_count = lax.axis_size("col")
    half_devices = row_count // 2
    panel = roots.shape[0]
    tiles = width // LANES
    vmem = pl.BlockSpec(memory_space=pltpu.VMEM)
    smem = pl.BlockSpec(memory_space=pltpu.SMEM)
    anywhere = pl.BlockSpec(memory_space=pl.ANY)
    limit = lambda mib: pltpu.CompilerParams(vmem_limit_bytes=mib * 2**20)
    in_hbm = lambda x: pltpu.with_memory_space_constraint(x, pltpu.HBM)
    square = lambda x: x.reshape(2, tiles, LANES).swapaxes(0, 1).reshape(2 * tiles, LANES)
    struct = jax.ShapeDtypeStruct
    roots = roots.reshape(1, -1)
    panel_source = panel_source.reshape(1, -1)
    shifts = square(shifts)
    deflate_mask = square(deflate_mask)
    lines = pl.pallas_call(
        functools.partial(pick_kernel, height=height),
        out_shape=struct((half_devices, tiles, LANES), eigvec_rows.dtype),
        in_specs=[smem, anywhere],
        out_specs=vmem,
        scratch_shapes=[pltpu.VMEM((ALIGN, width), eigvec_rows.dtype), pltpu.SemaphoreType.DMA],
        compiler_params=limit(4),
        name="pick_line",
    )(in_hbm(split), in_hbm(eigvec_rows))
    halves = [list(range(half_devices)), list(range(half_devices, row_count))]
    lines = lax.all_to_all(lines, "row", 0, 0, axis_index_groups=halves)
    square_struct = struct((panel, LANES), jnp.float32)
    row_struct = struct((SUBLANES, panel), jnp.float32)
    line_struct = struct((tiles, LANES), jnp.float32)
    norm, sums, kept, own_shifts, poles, unit = pl.pallas_call(
        functools.partial(norm_kernel, height=height, columns=width * col_count),
        out_shape=(row_struct, row_struct, line_struct, line_struct, square_struct, struct((panel, LANES), jnp.int32)),
        in_specs=[smem] + [vmem] * 6,
        out_specs=(vmem,) * 6,
        compiler_params=limit(12),
        name="column_norms",
    )(split, lines, eigvec_rows, shifts, deflate_mask, roots, panel_source)
    flip = half_devices + half_devices // 2
    other = lax.ppermute(norm, "row", [(i, i ^ flip) for i in range(row_count)])
    body = panel // col_count * height // LANES
    parts = pl.pallas_call(
        product_kernel,
        out_shape=struct((col_count, body + SUBLANES, LANES), jnp.float32),
        in_specs=[vmem] * 5,
        out_specs=vmem,
        compiler_params=limit(16),
        cost_estimate=pl.CostEstimate(flops=2 * 10**9, bytes_accessed=2**24, transcendentals=2**20),
        name="block_product",
    )(kept, own_shifts, poles, unit, eigvec_rows)
    extra = jnp.broadcast_to(sums + other, (col_count, SUBLANES, LANES))
    parts = lax.dynamic_update_slice(parts, extra, (0, body, 0))
    parts = lax.all_to_all(parts, "col", 0, 0)
    return pl.pallas_call(
        finish_kernel,
        out_shape=struct((panel // col_count, height), jnp.float32),
        in_specs=[vmem],
        out_specs=vmem,
        scratch_shapes=[pltpu.VMEM((panel, col_count * SUBLANES), jnp.float32)],
        compiler_params=limit(4),
        name="scale_and_add",
    )(parts)


def solution(mesh):
    return jax.shard_map(
        local,
        mesh=mesh,
        in_specs=(P("row", "col"), P(), P(None, "col"), P(), P(None, "col"), P()),
        out_specs=P("col", "row"),
        check_vma=False,
    )
```

time: 45.5 us -> 42.4 us (0.932)
  Pallas kernels: 9.44 us -> 7.14 us
  blocking collectives: 33.1 us -> 32.4 us
    pallas_call x3 -> x2, Pallas kernels: 6.44 us -> 4.04 us  [the longest x1 2.44 us: local(): pl.pallas_call(product_kernel, out_shape=struct((col_count, body + SUBLAN...]
    all_to_all x1, blocking collectives: 21.9 us -> 21.2 us  [local(): parts = lax.all_to_all(parts, 'col', 0, 0)]
  transfers between devices with their start and end apart: 1 -> 1, of which waited for: 0 -> 0; matrix products, arithmetic and copies ran while one was open for 0% -> 0% of each run, Pallas kernels for 7% -> 6%
where the time goes in v4:
time: 42.4 us; the launch traced here: 42.3 us
  blocking collectives  32.4 us (76%)
  Pallas kernels  7.14 us (17%)
  starting transfers between devices  2.54 us (6%)
    all_to_all x1, blocking collectives, local(): parts = lax.all_to_all(parts, 'col', 0, 0)  21.2 us
    all_to_all x1, blocking collectives, local(): lines = lax.all_to_all(lines, 'row', 0, 0, axis_index_groups=halves)  11.2 us
    ppermute x1, starting transfers between devices, local(): other = lax.ppermute(norm, 'row', [(i, i ^ flip) for i in range(row_count)])  2.54 us
    pallas_call x1, Pallas kernels, local(): pl.pallas_call(product_kernel, out_shape=struct((col_count, body + SUBLAN...  2.44 us
    pallas_call x1, Pallas kernels, local(): pl.pallas_call(functools.partial(pick_kernel, height=height), out_shape=s...  2.19 us
    pallas_call x1, Pallas kernels, local(): pl.pallas_call(functools.partial(norm_kernel, height=height, columns=widt...  1.6 us
    pallas_call x1, Pallas kernels, local(): pl.pallas_call(finish_kernel, out_shape=struct((panel // col_count, heigh...  0.91 us
  transfers between devices with their start and end apart: 1, of which 0 were waited for; matrix products, arithmetic and copies ran while one was open for 0% of the time, Pallas kernels for 6%

profile of v4, /device:TPU:8, one launch (start us, length us, event | category | flops | bytes accessed | tf_op | source)
XLA Modules:
  0.0 42.3 jit_solution(4115721684285859258)
XLA Ops:
  0.0 0.0 copy-start
  0.0 0.0 copy-start.3
  0.0 0.0 copy-start.5
  0.0 0.0 copy-start.2
  0.0 0.0 copy-start.4
  0.0 0.0 copy-start.1
  0.0 2.2 %pick_line.1 = bf16[16,64,128]{2,1,0:T(8,128)(2,1)S(1)} custom-call(s32[2]{0:T(128)} %split_ref.3, bf16[512,8192]{1,0:T(8,128)(2,1)} %rows_ref.3), custom_call_target="tpu_custom_call" | custom-call | tf_op jit(solution)/shard_map/pick_line/pallas_call | solution.py:150
  2.2 11.2 %all_to_all.10.lines_ref = bf16[16,64,128]{2,1,0:T(8,128)(2,1)S(1)} all-to-all(bf16[16,64,128]{2,1,0:T(8,128)(2,1)S(1)} %pick_line.1), channel_id=1, replica_groups={{0,8,16,24,32,40,48,56,64,72,80,88,96,104,112,120},{128,136,144,152,160..., dimensions={0} | all-to-all | bytes 524288 | tf_op jit(solution)/shard_map/all_to_all | solution.py:160
  13.5 0.0 copy-done
  13.5 0.0 copy-done.3
  13.5 0.0 copy-done.5
  13.5 0.0 copy-done.2
  13.5 0.0 copy-done.4
  13.5 0.0 copy-done.1
  13.5 1.6 %column_norms.1 = (f32[8,128]{1,0:T(8,128)S(1)}, f32[8,128]{1,0:T(8,128)S(1)}, f32[64,128]{1,0:T(8,128)S(1)}, f32[64,128]{1,0:T(8,128)S(1)}, f32[128,128]{1,0:T(8,128)S(1)}, /*index=5*/s32[128,128]{1,0:T(8,128)S(1)}) custom-call(s32[2]{0:T(128)S(1)} %copy-done.3, bf16[16,64,128]{2,1,0:T(8,128)(2,1)S(1)} %all_to_all.10.lines_ref, ...), custom_call_target="tpu_custom_call" | custom-call | tf_op jit(solution)/shard_map/column_norms/pallas_call | solution.py:164
  15.1 2.5 %collective-permute-start = (f32[8,128]{1,0:T(8,128)S(1)}, f32[8,128]{1,0:T(8,128)S(1)}, u32[]{:S(2)}, u32[]{:S(2)}) collective-permute-start(f32[8,128]{1,0:T(8,128)S(1)} %get-tuple-element.16), channel_id=1, source_target_pairs={{0,192},{8,200},{16,208},{24,216},{32,224},{40,232},{48,240},{56,2... | collective-permute-start | bytes 12296 | tf_op jit(solution)/shard_map/ppermute | solution.py:173
  17.7 2.4 %block_product.1 = f32[8,72,128]{2,1,0:T(8,128)S(1)} custom-call(f32[64,128]{1,0:T(8,128)S(1)} %get-tuple-element.11.kept_ref, f32[64,128]{1,0:T(8,128)S(1)} %get-tuple-element.12.shifts_ref, f32[128,128]{1,0:T(8,128)S(1)} %get-tuple-element.13.poles_ref, s32[128,128]{1,0:T(8,128)S(1)} %get-tuple-element.14.unit_ref, bf16[512,8192]{1,0:T(8,128)(2,1)S(1)} %copy-done), custom_call_target="tpu_custom_call" | custom-call | flops 2000000000 | bytes 16777216 | tf_op jit(solution)/shard_map/block_product/pallas_call | solution.py:175
  20.1 0.0 collective-permute-done
  20.1 21.2 %all_to_all.11.parts_ref = f32[8,72,128]{2,1,0:T(8,128)S(1)} all-to-all(f32[8,72,128]{2,1,0:T(8,128)S(1)} %broadcast_dynamic-update-slice_fusion), channel_id=1, replica_groups=mesh['row'=32,'col'=8] {'col'}, dimensions={0} | all-to-all | bytes 589824 | tf_op jit(solution)/shard_map/all_to_all | solution.py:186
  41.4 0.9 %scale_and_add.1 = f32[16,512]{1,0:T(8,128)} custom-call(f32[8,72,128]{2,1,0:T(8,128)S(1)} %all_to_all.11.parts_ref), custom_call_target="tpu_custom_call" | custom-call | tf_op jit(solution)/shard_map/scale_and_add/pallas_call | solution.py:187
  (2 shorter events, 0.0 us)
Async XLA Ops:
  0.0 13.5 %copy-start = (bf16[512,8192]{1,0:T(8,128)(2,1)S(1)}, bf16[512,8192]{1,0:T(8,128)(2,1)}, u32[]{:S(2)}) copy-start(bf16[512,8192]{1,0:T(8,128)(2,1)} %rows_ref.3) | copy-start | bytes 25165828
  0.0 13.5 %copy-start.3 = (s32[2]{0:T(128)S(1)}, s32[2]{0:T(128)}, u32[]{:S(2)}) copy-start(s32[2]{0:T(128)} %split_ref.3) | copy-start | bytes 28
  0.0 13.5 %copy-start.5 = (s32[128]{0:T(128)S(1)}, s32[128]{0:T(128)}, u32[]{:S(2)}) copy-start(s32[128]{0:T(128)} %param.11) | copy-start | bytes 1540
  0.0 13.5 %copy-start.2 = (s32[2,8192]{1,0:T(2,128)S(1)}, s32[2,8192]{1,0:T(2,128)}, u32[]{:S(2)}) copy-start(s32[2,8192]{1,0:T(2,128)} %param.10) | copy-start | bytes 196612
  0.0 13.5 %copy-start.4 = (f32[128]{0:T(128)S(1)}, f32[128]{0:T(128)}, u32[]{:S(2)}) copy-start(f32[128]{0:T(128)} %param.9) | copy-start | bytes 1540
  0.0 13.5 %copy-start.1 = (f32[2,8192]{1,0:T(2,128)S(1)}, f32[2,8192]{1,0:T(2,128)}, u32[]{:S(2)}) copy-start(f32[2,8192]{1,0:T(2,128)} %param.8) | copy-start | bytes 196612
  15.1 5.0 %collective-permute-start = (f32[8,128]{1,0:T(8,128)S(1)}, f32[8,128]{1,0:T(8,128)S(1)}, u32[]{:S(2)}, u32[]{:S(2)}) collective-permute-start(f32[8,128]{1,0:T(8,128)S(1)} %get-tuple-element.16), channel_id=1, source_target_pairs={{0,192},{8,200},{16,208},{24,216},{32,224},{40,232},{48,240},{56,2... | collective-permute-start | bytes 12296 | tf_op jit(solution)/shard_map/ppermute | solution.py:173

commit v5 on v4

v5 whole, which is shorter than its diff:
```python
import functools

import jax
import jax.numpy as jnp
from jax import lax
from jax.experimental import pallas as pl
from jax.experimental.pallas import tpu as pltpu
from jax.sharding import PartitionSpec as P

LANES = 128
ALIGN = 16
SUBLANES = 8
CHUNKS = 8
LOW_BLOCKS = 2


def spread(line):
    return jnp.broadcast_to(line, (LANES, line.shape[1])).T


def pick_kernel(
    split_hbm, rows_hbm, shifts_hbm, mask_hbm, roots_hbm, source_hbm,
    out_ref, own_mask_ref, own_shifts_ref, poles_ref, unit_ref, flags_ref, squares_ref,
    split_ref, window, shifts_ref, mask_ref, roots_ref, source_ref, sems, *, columns
):
    half = lax.axis_index("row") // (lax.axis_size("row") // 2)
    height, width = rows_hbm.shape
    panel = roots_ref.shape[1]
    tiles = width // LANES
    pairs = ((mask_hbm, mask_ref), (source_hbm, source_ref), (roots_hbm, roots_ref), (shifts_hbm, shifts_ref))
    split_copy = pltpu.make_async_copy(split_hbm, split_ref, sems.at[0])
    copies = [pltpu.make_async_copy(a, b, sems.at[i + 2]) for i, (a, b) in enumerate(pairs)]
    split_copy.start()
    for copy in copies:
        copy.start()
    split_copy.wait()
    row = split_ref[half] % height
    base = pl.multiple_of((row // ALIGN) * ALIGN, ALIGN)
    row_copy = pltpu.make_async_copy(rows_hbm.at[pl.ds(base, ALIGN)], window, sems.at[1])
    row_copy.start()
    for copy in copies:
        copy.wait()
    own_mask_ref[...] = mask_ref[pl.ds(half, tiles, stride=2), :]
    own_shifts_ref[...] = shifts_ref[pl.ds(half, tiles, stride=2), :]
    source = spread(source_ref[...])
    source_half = (source >= columns).astype(jnp.int32)
    local = source - source_half * columns - lax.axis_index("col") * width
    here = (local >= 0) & (local < width)
    lane = lax.broadcasted_iota(jnp.int32, (panel, LANES), 1)
    tile_of = jnp.where(here, local // LANES * 2 + source_half, -1)
    picked = jnp.dot(
        jnp.where(lax.broadcasted_iota(jnp.int32, (panel, 2 * tiles), 1) == tile_of[:, 0:1], 1.0, 0.0).astype(jnp.bfloat16),
        mask_ref[...].astype(jnp.float32).astype(jnp.bfloat16),
        preferred_element_type=jnp.float32,
    )
    deflated = jnp.sum(jnp.where(lane == local % LANES, picked, 0.0), axis=1, keepdims=True) > 0.5
    own_flag = deflated & (source_half == half)
    poles_ref[...] = jnp.where(own_flag, 3e38, spread(roots_ref[...]))
    unit_ref[...] = jnp.where(own_flag, local, -1)
    own = jnp.where(own_flag, 1.0, 0.0)
    other = jnp.where(deflated & (source_half != half), 1.0, 0.0)
    flags_ref[...] = jnp.where(lane == 1, own, jnp.where(lane == 2, other, 0.0)).T[0:SUBLANES]
    roots_all = spread(roots_ref[...])
    for t in range(tiles):
        inverse = pltpu.reciprocal(own_shifts_ref[t : t + 1, :] - roots_all, approx=True)
        squares_ref[:, t * LANES : (t + 1) * LANES] = inverse * inverse
    row_copy.wait()
    inner = row - base
    lower = inner < SUBLANES
    inner = lax.rem(inner, SUBLANES)
    sublane = lax.broadcasted_iota(jnp.int32, (SUBLANES, LANES), 0)
    blocks = [jnp.zeros((SUBLANES, LANES), jnp.float32) for _ in range(tiles // SUBLANES)]
    for t in range(tiles):
        both = window[:, t * LANES : (t + 1) * LANES].astype(jnp.float32)
        eight = jnp.where(lower, both[0:SUBLANES], both[SUBLANES:])
        target = t % SUBLANES
        turned = pltpu.roll(eight, lax.rem(target - inner + SUBLANES, SUBLANES), 0)
        blocks[t // SUBLANES] = jnp.where(sublane == target, turned, blocks[t // SUBLANES])
    line = jnp.concatenate(blocks, axis=0).astype(out_ref.dtype)
    for target in range(out_ref.shape[0]):
        out_ref[target] = line


def norm_kernel(
    split_ref, lines_ref, mask_ref, squares_ref, flags_ref, norm_ref, sums_ref, kept_ref, line_ref, *, height
):
    half = lax.axis_index("row") // (lax.axis_size("row") // 2)
    panel = squares_ref.shape[0]
    tiles = lines_ref.shape[1]
    line = lines_ref[split_ref[half] // height].astype(jnp.float32)
    kept = jnp.where(mask_ref[...] == 1, 0.0, line)
    kept_ref[...] = kept
    line_ref[...] = kept * kept
    norm = jnp.zeros((panel, LANES), jnp.float32)
    for t in range(tiles):
        norm = norm + line_ref[t : t + 1, :] * squares_ref[:, t * LANES : (t + 1) * LANES]
    lane = lax.broadcasted_iota(jnp.int32, (panel, LANES), 1)
    norm = jnp.where(lane == 0, jnp.sum(norm, axis=1, keepdims=True), 0.0).T[0:SUBLANES]
    norm_ref[...] = norm
    sums_ref[...] = norm + flags_ref[...]


def product_kernel(kept_ref, shifts_ref, poles_ref, unit_ref, rows_ref, out_ref):
    panel = poles_ref.shape[0]
    groups = out_ref.shape[0]
    per_group = panel // groups
    height, width = rows_ref.shape
    poles = poles_ref[...]
    unit = unit_ref[...]
    lane = lax.broadcasted_iota(jnp.int32, (1, LANES), 1)
    total = jnp.zeros((2 * panel, height), jnp.float32)
    chunk = width // CHUNKS
    for c in range(CHUNKS):
        highs, lows = [], []
        for t in range(c * chunk // LANES, (c + 1) * chunk // LANES):
            cauchy = kept_ref[t : t + 1, :] * pltpu.reciprocal(shifts_ref[t : t + 1, :] - poles, approx=True)
            value = jnp.where(unit == lane + t * LANES, 1.0, cauchy)
            high = value.astype(jnp.bfloat16)
            highs.append(high)
            lows.append((value - high.astype(jnp.float32)).astype(jnp.bfloat16))
        merged = jnp.concatenate([jnp.concatenate(highs, axis=1), jnp.concatenate(lows, axis=1)], axis=0)
        total = total + lax.dot_general(
            merged, rows_ref[:, c * chunk : (c + 1) * chunk], (((1,), (1,)), ((), ())),
            preferred_element_type=jnp.float32,
        )
    product = (total[0:panel] + total[panel : 2 * panel]).reshape(groups, per_group, height)
    blocks = height // LANES
    for q in range(blocks):
        block = product[:, :, q * LANES : (q + 1) * LANES]
        high = block.astype(jnp.bfloat16)
        out_ref[:, q * per_group : (q + 1) * per_group, :] = high
        if q < LOW_BLOCKS:
            low = (block - high.astype(jnp.float32)).astype(jnp.bfloat16)
            out_ref[:, (blocks + q) * per_group : (blocks + q + 1) * per_group, :] = low
    extra = (blocks + LOW_BLOCKS) * per_group
    out_ref[:, extra:, :] = jnp.zeros((groups, ALIGN, LANES), jnp.bfloat16)


def finish_kernel(parts_ref, out_ref, columns_ref):
    groups = parts_ref.shape[0]
    per_group, height = out_ref.shape
    blocks = height // LANES
    extra = (blocks + LOW_BLOCKS) * per_group
    columns_ref[...] = parts_ref[:, extra:, :].astype(jnp.float32).reshape(groups * ALIGN, LANES).T
    start = pl.multiple_of(lax.axis_index("col") * per_group, per_group)
    sums = columns_ref[pl.ds(start, per_group), :]
    kind = lax.broadcasted_iota(jnp.int32, sums.shape, 1) % ALIGN
    total = lambda chosen: jnp.sum(jnp.where(chosen, sums, 0.0), axis=1, keepdims=True)
    norm2, own, other = total((kind == 0) | (kind == SUBLANES)), total(kind == 1), total(kind == 2)
    scale = 1.0 / jnp.sqrt(norm2)
    results = [jnp.zeros((per_group, LANES), jnp.float32) for _ in range(blocks)]
    for group in range(groups):
        flag = sums[:, group * ALIGN + 1 : group * ALIGN + 2]
        weight = jnp.where(own + other > 0.5, flag, scale)
        for q in range(blocks):
            value = parts_ref[group, q * per_group : (q + 1) * per_group, :].astype(jnp.float32)
            if q < LOW_BLOCKS:
                low = parts_ref[group, (blocks + q) * per_group : (blocks + q + 1) * per_group, :]
                value = value + low.astype(jnp.float32)
            results[q] = results[q] + weight * value
    for q in range(blocks):
        out_ref[:, q * LANES : (q + 1) * LANES] = jnp.where(other > 0.5, 0.0, results[q])


def local(eigvec_rows, split, shifts, roots, deflate_mask, panel_source):
    height, width = eigvec_rows.shape
    row_count = lax.axis_size("row")
    col_count = lax.axis_size("col")
    half_devices = row_count // 2
    panel = roots.shape[0]
    tiles = width // LANES
    vmem = pl.BlockSpec(memory_space=pltpu.VMEM)
    smem = pl.BlockSpec(memory_space=pltpu.SMEM)
    anywhere = pl.BlockSpec(memory_space=pl.ANY)
    limit = lambda mib: pltpu.CompilerParams(vmem_limit_bytes=mib * 2**20)
    in_hbm = lambda x: pltpu.with_memory_space_constraint(x, pltpu.HBM)
    square = lambda x: x.reshape(2, tiles, LANES).swapaxes(0, 1).reshape(2 * tiles, LANES)
    struct = jax.ShapeDtypeStruct
    roots = roots.reshape(1, -1)
    panel_source = panel_source.reshape(1, -1)
    shifts = square(shifts)
    deflate_mask = square(deflate_mask)
    row_struct = struct((SUBLANES, panel), jnp.float32)
    line_struct = lambda kind: struct((tiles, LANES), kind)
    square_struct = lambda kind: struct((panel, LANES), kind)
    lines, own_mask, own_shifts, poles, unit, flags, squares = pl.pallas_call(
        functools.partial(pick_kernel, columns=width * col_count),
        out_shape=(
            struct((half_devices, tiles, LANES), eigvec_rows.dtype),
            line_struct(jnp.int32),
            line_struct(jnp.float32),
            square_struct(jnp.float32),
            square_struct(jnp.int32),
            row_struct,
            struct((panel, width), jnp.float32),
        ),
        in_specs=[anywhere] * 6,
        out_specs=(vmem,) * 7,
        scratch_shapes=[
            pltpu.SMEM((2,), jnp.int32),
            pltpu.VMEM((ALIGN, width), eigvec_rows.dtype),
            pltpu.VMEM((2 * tiles, LANES), jnp.float32),
            pltpu.VMEM((2 * tiles, LANES), jnp.int32),
            pltpu.VMEM((1, panel), jnp.float32),
            pltpu.VMEM((1, panel), jnp.int32),
            pltpu.SemaphoreType.DMA((6,)),
        ],
        compiler_params=limit(4),
        name="pick_line",
    )(*[in_hbm(x) for x in (split, eigvec_rows, shifts, deflate_mask, roots, panel_source)])
    halves = [list(range(half_devices)), list(range(half_devices, row_count))]
    lines = lax.all_to_all(lines, "row", 0, 0, axis_index_groups=halves)
    norm, sums, kept = pl.pallas_call(
        functools.partial(norm_kernel, height=height),
        out_shape=(row_struct, row_struct, line_struct(jnp.float32)),
        in_specs=[smem] + [vmem] * 4,
        out_specs=(vmem,) * 3,
        scratch_shapes=[pltpu.VMEM((tiles, LANES), jnp.float32)],
        compiler_params=limit(8),
        name="column_norms",
    )(split, lines, own_mask, squares, flags)
    flip = half_devices + half_devices // 2
    other = lax.ppermute(norm, "row", [(i, i ^ flip) for i in range(row_count)])
    body = panel // col_count * (height // LANES + LOW_BLOCKS)
    parts = pl.pallas_call(
        product_kernel,
        out_shape=struct((col_count, body + ALIGN, LANES), jnp.bfloat16),
        in_specs=[vmem] * 5,
        out_specs=vmem,
        compiler_params=limit(16),
        cost_estimate=pl.CostEstimate(flops=2 * 10**9, bytes_accessed=2**24, transcendentals=2**20),
        name="block_product",
    )(kept, own_shifts, poles, unit, eigvec_rows)
    norms = sums + other
    first = lax.reduce_precision(norms, 8, 7)
    extra = jnp.concatenate([first, norms - first]).astype(jnp.bfloat16)
    extra = jnp.broadcast_to(extra, (col_count, ALIGN, LANES))
    parts = lax.dynamic_update_slice(parts, extra, (0, body, 0))
    parts = lax.all_to_all(parts, "col", 0, 0)
    return pl.pallas_call(
        finish_kernel,
        out_shape=struct((panel // col_count, height), jnp.float32),
        in_specs=[vmem],
        out_specs=vmem,
        scratch_shapes=[pltpu.VMEM((panel, col_count * ALIGN), jnp.float32)],
        compiler_params=limit(4),
        name="scale_and_add",
    )(parts)


def solution(mesh):
    return jax.shard_map(
        local,
        mesh=mesh,
        in_specs=(P("row", "col"), P(), P(None, "col"), P(), P(None, "col"), P()),
        out_specs=P("col", "row"),
        check_vma=False,
    )
```

time: 42.4 us -> 40.5 us (0.955)
  blocking collectives: 32.4 us -> 31 us
  Pallas kernels: 7.14 us -> 6.7 us
    all_to_all x1, blocking collectives: 21.2 us -> 19.8 us  [local(): parts = lax.all_to_all(parts, 'col', 0, 0)]
    pallas_call x3, Pallas kernels: 6.23 us -> 5.79 us  [the longest x1 2.36 us: local(): pl.pallas_call(product_kernel, out_shape=struct((col_count, body + ALIGN,...]
where the time goes in v5:
time: 40.5 us; the launch traced here: 40.4 us
  blocking collectives  31 us (77%)
  Pallas kernels  6.7 us (17%)
  starting transfers between devices  2.56 us (6%)
    all_to_all x1, blocking collectives, local(): parts = lax.all_to_all(parts, 'col', 0, 0)  19.8 us
    all_to_all x1, blocking collectives, local(): lines = lax.all_to_all(lines, 'row', 0, 0, axis_index_groups=halves)  11.2 us
    ppermute x1, starting transfers between devices, local(): other = lax.ppermute(norm, 'row', [(i, i ^ flip) for i in range(row_count)])  2.56 us
    pallas_call x1, Pallas kernels, local(): pl.pallas_call(product_kernel, out_shape=struct((col_count, body + ALIGN,...  2.36 us
    pallas_call x1, Pallas kernels, local(): pl.pallas_call(functools.partial(pick_kernel, columns=width * col_count),...  2.33 us
    pallas_call x1, Pallas kernels, local(): pl.pallas_call(functools.partial(norm_kernel, height=height), out_shape=(...  1.1 us
    pallas_call x1, Pallas kernels, local(): pl.pallas_call(finish_kernel, out_shape=struct((panel // col_count, heigh...  0.91 us
  transfers between devices with their start and end apart: 1, of which 0 were waited for; matrix products, arithmetic and copies ran while one was open for 0% of the time, Pallas kernels for 6%

profile of v5, /device:TPU:8, one launch (start us, length us, event | category | flops | bytes accessed | tf_op | source)
XLA Modules:
  0.0 40.4 jit_solution(11594276526290444457)
XLA Ops:
  0.0 0.0 copy-start.1
  0.0 0.0 copy-start
  0.0 2.3 %pick_line.1 = (bf16[16,64,128]{2,1,0:T(8,128)(2,1)S(1)}, s32[64,128]{1,0:T(8,128)S(1)}, f32[64,128]{1,0:T(8,128)S(1)}, f32[128,128]{1,0:T(8,128)S(1)}, s32[128,...) custom-call(s32[2]{0:T(128)} %split_ref.1, bf16[512,8192]{1,0:T(8,128)(2,1)} %rows_ref.1, ...), custom_call_target="tpu_custom_call" | custom-call | tf_op jit(solution)/shard_map/pick_line/pallas_call | solution.py:186
  2.3 11.2 %all_to_all.10.lines_ref = bf16[16,64,128]{2,1,0:T(8,128)(2,1)S(1)} all-to-all(bf16[16,64,128]{2,1,0:T(8,128)(2,1)S(1)} %get-tuple-element.15), channel_id=1, replica_groups={{0,8,16,24,32,40,48,56,64,72,80,88,96,104,112,120},{128,136,144,152,160..., dimensions={0} | all-to-all | bytes 524288 | tf_op jit(solution)/shard_map/all_to_all | solution.py:212
  13.6 0.0 copy-done.1
  13.6 1.1 %column_norms.1 = (f32[8,128]{1,0:T(8,128)S(1)}, f32[8,128]{1,0:T(8,128)S(1)}, f32[64,128]{1,0:T(8,128)S(1)}) custom-call(s32[2]{0:T(128)S(1)} %copy-done.1, bf16[16,64,128]{2,1,0:T(8,128)(2,1)S(1)} %all_to_all.10.lines_ref, s32[64,128]{1,0:T(8,128)S(1)} %get-tuple-element.16.mask_ref, f32[128,8192]{1,0:T(8,128)S(1)} %get-tuple-element.17.squares_ref, ...), custom_call_target="tpu_custom_call" | custom-call | tf_op jit(solution)/shard_map/column_norms/pallas_call | solution.py:213
  14.7 2.6 %collective-permute-start = (f32[8,128]{1,0:T(8,128)S(1)}, f32[8,128]{1,0:T(8,128)S(1)}, u32[]{:S(2)}, u32[]{:S(2)}) collective-permute-start(f32[8,128]{1,0:T(8,128)S(1)} %get-tuple-element.24), channel_id=1, source_target_pairs={{0,192},{8,200},{16,208},{24,216},{32,224},{40,232},{48,240},{56,2... | collective-permute-start | bytes 12296 | tf_op jit(solution)/shard_map/ppermute | solution.py:223
  17.2 0.0 copy-done
  17.2 2.4 %block_product.1 = bf16[8,112,128]{2,1,0:T(8,128)(2,1)S(1)} custom-call(f32[64,128]{1,0:T(8,128)S(1)} %get-tuple-element.19.kept_ref, f32[64,128]{1,0:T(8,128)S(1)} %get-tuple-element.20.shifts_ref, f32[128,128]{1,0:T(8,128)S(1)} %get-tuple-element.21.poles_ref, s32[128,128]{1,0:T(8,128)S(1)} %get-tuple-element.22.unit_ref, bf16[512,8192]{1,0:T(8,128)(2,1)S(1)} %copy-done), custom_call_target="tpu_custom_call" | custom-call | flops 2000000000 | bytes 16777216 | tf_op jit(solution)/shard_map/block_product/pallas_call | solution.py:225
  19.6 0.0 collective-permute-done
  19.7 19.8 %all_to_all.11.parts_ref = bf16[8,112,128]{2,1,0:T(8,128)(2,1)S(1)} all-to-all(bf16[8,112,128]{2,1,0:T(8,128)(2,1)S(1)} %broadcast_dynamic-update-slice_fusion), channel_id=1, replica_groups=mesh['row'=32,'col'=8] {'col'}, dimensions={0} | all-to-all | bytes 458752 | tf_op jit(solution)/shard_map/all_to_all | solution.py:239
  39.5 0.9 %scale_and_add.1 = f32[16,512]{1,0:T(8,128)} custom-call(bf16[8,112,128]{2,1,0:T(8,128)(2,1)S(1)} %all_to_all.11.parts_ref), custom_call_target="tpu_custom_call" | custom-call | tf_op jit(solution)/shard_map/scale_and_add/pallas_call | solution.py:240
  (3 shorter events, 0.0 us)
Async XLA Ops:
  0.0 13.6 %copy-start.1 = (s32[2]{0:T(128)S(1)}, s32[2]{0:T(128)}, u32[]{:S(2)}) copy-start(s32[2]{0:T(128)} %split_ref.1) | copy-start | bytes 28
  0.0 17.2 %copy-start = (bf16[512,8192]{1,0:T(8,128)(2,1)S(1)}, bf16[512,8192]{1,0:T(8,128)(2,1)}, u32[]{:S(2)}) copy-start(bf16[512,8192]{1,0:T(8,128)(2,1)} %rows_ref.1) | copy-start | bytes 25165828
  14.7 4.9 %collective-permute-start = (f32[8,128]{1,0:T(8,128)S(1)}, f32[8,128]{1,0:T(8,128)S(1)}, u32[]{:S(2)}, u32[]{:S(2)}) collective-permute-start(f32[8,128]{1,0:T(8,128)S(1)} %get-tuple-element.24), channel_id=1, source_target_pairs={{0,192},{8,200},{16,208},{24,216},{32,224},{40,232},{48,240},{56,2... | collective-permute-start | bytes 12296 | tf_op jit(solution)/shard_map/ppermute | solution.py:223

commit v6 on v5

--- a/solution.py
+++ b/solution.py
@@ -20,7 +20,7 @@
 
 def pick_kernel(
     split_hbm, rows_hbm, shifts_hbm, mask_hbm, roots_hbm, source_hbm,
-    out_ref, own_mask_ref, own_shifts_ref, poles_ref, unit_ref, flags_ref, squares_ref,
+    out_ref, own_mask_ref, own_shifts_ref, poles_ref, unit_ref, flags_ref, squares_ref, holder_ref,
     split_ref, window, shifts_ref, mask_ref, roots_ref, source_ref, sems, *, columns
 ):
     half = lax.axis_index("row") // (lax.axis_size("row") // 2)
@@ -35,6 +35,8 @@
         copy.start()
     split_copy.wait()
     row = split_ref[half] % height
+    device = lax.broadcasted_iota(jnp.int32, holder_ref.shape, 0)
+    holder_ref[...] = jnp.where(device == split_ref[half] // height, 1.0, 0.0)
     base = pl.multiple_of((row // ALIGN) * ALIGN, ALIGN)
     row_copy = pltpu.make_async_copy(rows_hbm.at[pl.ds(base, ALIGN)], window, sems.at[1])
     row_copy.start()
@@ -82,12 +84,13 @@
 
 
 def norm_kernel(
-    split_ref, lines_ref, mask_ref, squares_ref, flags_ref, norm_ref, sums_ref, kept_ref, line_ref, *, height
+    holder_ref, lines_ref, mask_ref, squares_ref, flags_ref, norm_ref, sums_ref, kept_ref, line_ref
 ):
-    half = lax.axis_index("row") // (lax.axis_size("row") // 2)
     panel = squares_ref.shape[0]
     tiles = lines_ref.shape[1]
-    line = lines_ref[split_ref[half] // height].astype(jnp.float32)
+    line = jnp.zeros((tiles, LANES), jnp.float32)
+    for device in range(lines_ref.shape[0]):
+        line = jnp.where(holder_ref[device : device + 1, :] > 0.5, lines_ref[device].astype(jnp.float32), line)
     kept = jnp.where(mask_ref[...] == 1, 0.0, line)
     kept_ref[...] = kept
     line_ref[...] = kept * kept
@@ -170,7 +173,6 @@
     panel = roots.shape[0]
     tiles = width // LANES
     vmem = pl.BlockSpec(memory_space=pltpu.VMEM)
-    smem = pl.BlockSpec(memory_space=pltpu.SMEM)
     anywhere = pl.BlockSpec(memory_space=pl.ANY)
     limit = lambda mib: pltpu.CompilerParams(vmem_limit_bytes=mib * 2**20)
     in_hbm = lambda x: pltpu.with_memory_space_constraint(x, pltpu.HBM)
@@ -183,7 +185,7 @@
     row_struct = struct((SUBLANES, panel), jnp.float32)
     line_struct = lambda kind: struct((tiles, LANES), kind)
     square_struct = lambda kind: struct((panel, LANES), kind)
-    lines, own_mask, own_shifts, poles, unit, flags, squares = pl.pallas_call(
+    lines, own_mask, own_shifts, poles, unit, flags, squares, holder = pl.pallas_call(
         functools.partial(pick_kernel, columns=width * col_count),
         out_shape=(
             struct((half_devices, tiles, LANES), eigvec_rows.dtype),
@@ -193,9 +195,10 @@
             square_struct(jnp.int32),
             row_struct,
             struct((panel, width), jnp.float32),
+            struct((half_devices, LANES), jnp.float32),
         ),
         in_specs=[anywhere] * 6,
-        out_specs=(vmem,) * 7,
+        out_specs=(vmem,) * 8,
         scratch_shapes=[
             pltpu.SMEM((2,), jnp.int32),
             pltpu.VMEM((ALIGN, width), eigvec_rows.dtype),
@@ -211,14 +214,14 @@
     halves = [list(range(half_devices)), list(range(half_devices, row_count))]
     lines = lax.all_to_all(lines, "row", 0, 0, axis_index_groups=halves)
     norm, sums, kept = pl.pallas_call(
-        functools.partial(norm_kernel, height=height),
+        norm_kernel,
         out_shape=(row_struct, row_struct, line_struct(jnp.float32)),
-        in_specs=[smem] + [vmem] * 4,
+        in_specs=[vmem] * 5,
         out_specs=(vmem,) * 3,
         scratch_shapes=[pltpu.VMEM((tiles, LANES), jnp.float32)],
         compiler_params=limit(8),
         name="column_norms",
-    )(split, lines, own_mask, squares, flags)
+    )(holder, lines, own_mask, squares, flags)
     flip = half_devices + half_devices // 2
     other = lax.ppermute(norm, "row", [(i, i ^ flip) for i in range(row_count)])
     body = panel // col_count * (height // LANES + LOW_BLOCKS)

time: 40.5 us -> 39.5 us (0.975)
  Pallas kernels: 6.7 us -> 5.72 us
    pallas_call x1, Pallas kernels: 1.1 us -> 0.46 us  [local(): pl.pallas_call(norm_kernel, out_shape=(row_struct, row_struct, line_struc...]
where the time goes in v6:
time: 39.5 us; the launch traced here: 39.4 us
  blocking collectives  31 us (78%)
  Pallas kernels  5.72 us (14%)
  starting transfers between devices  2.56 us (6%)
    all_to_all x1, blocking collectives, local(): parts = lax.all_to_all(parts, 'col', 0, 0)  19.8 us
    all_to_all x1, blocking collectives, local(): lines = lax.all_to_all(lines, 'row', 0, 0, axis_index_groups=halves)  11.2 us
    ppermute x1, starting transfers between devices, local(): other = lax.ppermute(norm, 'row', [(i, i ^ flip) for i in range(row_count)])  2.56 us
    pallas_call x1, Pallas kernels, local(): pl.pallas_call(product_kernel, out_shape=struct((col_count, body + ALIGN,...  2.36 us
    pallas_call x1, Pallas kernels, local(): pl.pallas_call(functools.partial(pick_kernel, columns=width * col_count),...  1.99 us
    pallas_call x1, Pallas kernels, local(): pl.pallas_call(finish_kernel, out_shape=struct((panel // col_count, heigh...  0.91 us
  transfers between devices with their start and end apart: 1, of which 0 were waited for; matrix products, arithmetic and copies ran while one was open for 0% of the time, Pallas kernels for 6%

profile of v6, /device:TPU:8, one launch (start us, length us, event | category | flops | bytes accessed | tf_op | source)
XLA Modules:
  0.0 39.4 jit_solution(10014056173455705632)
XLA Ops:
  0.0 0.0 copy-start
  0.0 2.0 %pick_line.1 = (bf16[16,64,128]{2,1,0:T(8,128)(2,1)S(1)}, s32[64,128]{1,0:T(8,128)S(1)}, f32[64,128]{1,0:T(8,128)S(1)}, f32[128,128]{1,0:T(8,128)S(1)}, s32[128,...) custom-call(s32[2]{0:T(128)} %split_hbm.1, ...), custom_call_target="tpu_custom_call" | custom-call | tf_op jit(solution)/shard_map/pick_line/pallas_call | solution.py:188
  2.0 11.2 %all_to_all.10.lines_ref = bf16[16,64,128]{2,1,0:T(8,128)(2,1)S(1)} all-to-all(bf16[16,64,128]{2,1,0:T(8,128)(2,1)S(1)} %get-tuple-element.17), channel_id=1, replica_groups={{0,8,16,24,32,40,48,56,64,72,80,88,96,104,112,120},{128,136,144,152,160..., dimensions={0} | all-to-all | bytes 524288 | tf_op jit(solution)/shard_map/all_to_all | solution.py:215
  13.2 0.5 %column_norms.1 = (f32[8,128]{1,0:T(8,128)S(1)}, f32[8,128]{1,0:T(8,128)S(1)}, f32[64,128]{1,0:T(8,128)S(1)}) custom-call(f32[16,128]{1,0:T(8,128)S(1)} %get-tuple-element.16.holder_ref, bf16[16,64,128]{2,1,0:T(8,128)(2,1)S(1)} %all_to_all.10.lines_ref, s32[64,128]{1,0:T(8,128)S(1)} %get-tuple-element.18.mask_ref, ...), custom_call_target="tpu_custom_call" | custom-call | tf_op jit(solution)/shard_map/column_norms/pallas_call | solution.py:216
  13.7 2.6 %collective-permute-start = (f32[8,128]{1,0:T(8,128)S(1)}, f32[8,128]{1,0:T(8,128)S(1)}, u32[]{:S(2)}, u32[]{:S(2)}) collective-permute-start(f32[8,128]{1,0:T(8,128)S(1)} %get-tuple-element.26), channel_id=1, source_target_pairs={{0,192},{8,200},{16,208},{24,216},{32,224},{40,232},{48,240},{56,2... | collective-permute-start | bytes 12296 | tf_op jit(solution)/shard_map/ppermute | solution.py:226
  16.3 0.0 copy-done
  16.3 2.4 %block_product.1 = bf16[8,112,128]{2,1,0:T(8,128)(2,1)S(1)} custom-call(f32[64,128]{1,0:T(8,128)S(1)} %get-tuple-element.21.kept_ref, f32[64,128]{1,0:T(8,128)S(1)} %get-tuple-element.22.shifts_ref, f32[128,128]{1,0:T(8,128)S(1)} %get-tuple-element.23.poles_ref, s32[128,128]{1,0:T(8,128)S(1)} %get-tuple-element.24.unit_ref, bf16[512,8192]{1,0:T(8,128)(2,1)S(1)} %copy-done), custom_call_target="tpu_custom_call" | custom-call | flops 2000000000 | bytes 16777216 | tf_op jit(solution)/shard_map/block_product/pallas_call | solution.py:228
  18.6 0.0 collective-permute-done
  18.7 19.8 %all_to_all.11.parts_ref = bf16[8,112,128]{2,1,0:T(8,128)(2,1)S(1)} all-to-all(bf16[8,112,128]{2,1,0:T(8,128)(2,1)S(1)} %broadcast_dynamic-update-slice_fusion), channel_id=1, replica_groups=mesh['row'=32,'col'=8] {'col'}, dimensions={0} | all-to-all | bytes 458752 | tf_op jit(solution)/shard_map/all_to_all | solution.py:242
  38.5 0.9 %scale_and_add.1 = f32[16,512]{1,0:T(8,128)} custom-call(bf16[8,112,128]{2,1,0:T(8,128)(2,1)S(1)} %all_to_all.11.parts_ref), custom_call_target="tpu_custom_call" | custom-call | tf_op jit(solution)/shard_map/scale_and_add/pallas_call | solution.py:243
  (3 shorter events, 0.0 us)
Async XLA Ops:
  0.0 16.3 %copy-start = (bf16[512,8192]{1,0:T(8,128)(2,1)S(1)}, bf16[512,8192]{1,0:T(8,128)(2,1)}, u32[]{:S(2)}) copy-start(bf16[512,8192]{1,0:T(8,128)(2,1)} %rows_ref.1) | copy-start | bytes 25165828
  13.7 4.9 %collective-permute-start = (f32[8,128]{1,0:T(8,128)S(1)}, f32[8,128]{1,0:T(8,128)S(1)}, u32[]{:S(2)}, u32[]{:S(2)}) collective-permute-start(f32[8,128]{1,0:T(8,128)S(1)} %get-tuple-element.26), channel_id=1, source_target_pairs={{0,192},{8,200},{16,208},{24,216},{32,224},{40,232},{48,240},{56,2... | collective-permute-start | bytes 12296 | tf_op jit(solution)/shard_map/ppermute | solution.py:226

commit v7 on v6

--- a/solution.py
+++ b/solution.py
@@ -144,17 +144,17 @@
     per_group, height = out_ref.shape
     blocks = height // LANES
     extra = (blocks + LOW_BLOCKS) * per_group
-    columns_ref[...] = parts_ref[:, extra:, :].astype(jnp.float32).reshape(groups * ALIGN, LANES).T
+    rows = parts_ref[:, extra:, :].astype(jnp.float32)
+    total = jnp.sum(rows, axis=0)
+    norm2, own, other = total[0:1] + total[SUBLANES : SUBLANES + 1], total[1:2], total[2:3]
+    scale = jnp.where(other > 0.5, 0.0, 1.0 / jnp.sqrt(norm2))
+    weights = [jnp.where(own > 0.5, rows[group, 1:2], scale) for group in range(groups)]
+    columns_ref[...] = jnp.concatenate(weights, axis=0).T
     start = pl.multiple_of(lax.axis_index("col") * per_group, per_group)
-    sums = columns_ref[pl.ds(start, per_group), :]
-    kind = lax.broadcasted_iota(jnp.int32, sums.shape, 1) % ALIGN
-    total = lambda chosen: jnp.sum(jnp.where(chosen, sums, 0.0), axis=1, keepdims=True)
-    norm2, own, other = total((kind == 0) | (kind == SUBLANES)), total(kind == 1), total(kind == 2)
-    scale = 1.0 / jnp.sqrt(norm2)
+    weights = columns_ref[pl.ds(start, per_group), :]
     results = [jnp.zeros((per_group, LANES), jnp.float32) for _ in range(blocks)]
     for group in range(groups):
-        flag = sums[:, group * ALIGN + 1 : group * ALIGN + 2]
-        weight = jnp.where(own + other > 0.5, flag, scale)
+        weight = weights[:, group : group + 1]
         for q in range(blocks):
             value = parts_ref[group, q * per_group : (q + 1) * per_group, :].astype(jnp.float32)
             if q < LOW_BLOCKS:
@@ -162,7 +162,7 @@
                 value = value + low.astype(jnp.float32)
             results[q] = results[q] + weight * value
     for q in range(blocks):
-        out_ref[:, q * LANES : (q + 1) * LANES] = jnp.where(other > 0.5, 0.0, results[q])
+        out_ref[:, q * LANES : (q + 1) * LANES] = results[q]
 
 
 def local(eigvec_rows, split, shifts, roots, deflate_mask, panel_source):
@@ -245,7 +245,7 @@
         out_shape=struct((panel // col_count, height), jnp.float32),
         in_specs=[vmem],
         out_specs=vmem,
-        scratch_shapes=[pltpu.VMEM((panel, col_count * ALIGN), jnp.float32)],
+        scratch_shapes=[pltpu.VMEM((panel, col_count), jnp.float32)],
         compiler_params=limit(4),
         name="scale_and_add",
     )(parts)

time: 39.5 us -> 39.5 us (level)
  no operation moved by 1% of the time
where the time goes in v7:
time: 39.5 us; the launch traced here: 39.3 us
  blocking collectives  31 us (78%)
  Pallas kernels  5.66 us (14%)
  starting transfers between devices  2.56 us (6%)
    all_to_all x1, blocking collectives, local(): parts = lax.all_to_all(parts, 'col', 0, 0)  19.8 us
    all_to_all x1, blocking collectives, local(): lines = lax.all_to_all(lines, 'row', 0, 0, axis_index_groups=halves)  11.2 us
    ppermute x1, starting transfers between devices, local(): other = lax.ppermute(norm, 'row', [(i, i ^ flip) for i in range(row_count)])  2.56 us
    pallas_call x1, Pallas kernels, local(): pl.pallas_call(product_kernel, out_shape=struct((col_count, body + ALIGN,...  2.36 us
    pallas_call x1, Pallas kernels, local(): pl.pallas_call(functools.partial(pick_kernel, columns=width * col_count),...  1.99 us
    pallas_call x1, Pallas kernels, local(): pl.pallas_call(finish_kernel, out_shape=struct((panel // col_count, heigh...  0.85 us
  transfers between devices with their start and end apart: 1, of which 0 were waited for; matrix products, arithmetic and copies ran while one was open for 0% of the time, Pallas kernels for 6%

profile of v7, /device:TPU:8, one launch (start us, length us, event | category | flops | bytes accessed | tf_op | source)
XLA Modules:
  0.0 39.3 jit_solution(17044725035203379780)
XLA Ops:
  0.0 0.0 copy-start
  0.0 2.0 %pick_line.1 = (bf16[16,64,128]{2,1,0:T(8,128)(2,1)S(1)}, s32[64,128]{1,0:T(8,128)S(1)}, f32[64,128]{1,0:T(8,128)S(1)}, f32[128,128]{1,0:T(8,128)S(1)}, s32[128,...) custom-call(s32[2]{0:T(128)} %split_hbm.1, ...), custom_call_target="tpu_custom_call" | custom-call | tf_op jit(solution)/shard_map/pick_line/pallas_call | solution.py:188
  2.0 11.2 %all_to_all.10.lines_ref = bf16[16,64,128]{2,1,0:T(8,128)(2,1)S(1)} all-to-all(bf16[16,64,128]{2,1,0:T(8,128)(2,1)S(1)} %get-tuple-element.17), channel_id=1, replica_groups={{0,8,16,24,32,40,48,56,64,72,80,88,96,104,112,120},{128,136,144,152,160..., dimensions={0} | all-to-all | bytes 524288 | tf_op jit(solution)/shard_map/all_to_all | solution.py:215
  13.2 0.5 %column_norms.1 = (f32[8,128]{1,0:T(8,128)S(1)}, f32[8,128]{1,0:T(8,128)S(1)}, f32[64,128]{1,0:T(8,128)S(1)}) custom-call(f32[16,128]{1,0:T(8,128)S(1)} %get-tuple-element.16.holder_ref, bf16[16,64,128]{2,1,0:T(8,128)(2,1)S(1)} %all_to_all.10.lines_ref, s32[64,128]{1,0:T(8,128)S(1)} %get-tuple-element.18.mask_ref, ...), custom_call_target="tpu_custom_call" | custom-call | tf_op jit(solution)/shard_map/column_norms/pallas_call | solution.py:216
  13.7 2.6 %collective-permute-start = (f32[8,128]{1,0:T(8,128)S(1)}, f32[8,128]{1,0:T(8,128)S(1)}, u32[]{:S(2)}, u32[]{:S(2)}) collective-permute-start(f32[8,128]{1,0:T(8,128)S(1)} %get-tuple-element.26), channel_id=1, source_target_pairs={{0,192},{8,200},{16,208},{24,216},{32,224},{40,232},{48,240},{56,2... | collective-permute-start | bytes 12296 | tf_op jit(solution)/shard_map/ppermute | solution.py:226
  16.3 0.0 copy-done
  16.3 2.4 %block_product.1 = bf16[8,112,128]{2,1,0:T(8,128)(2,1)S(1)} custom-call(f32[64,128]{1,0:T(8,128)S(1)} %get-tuple-element.21.kept_ref, f32[64,128]{1,0:T(8,128)S(1)} %get-tuple-element.22.shifts_ref, f32[128,128]{1,0:T(8,128)S(1)} %get-tuple-element.23.poles_ref, s32[128,128]{1,0:T(8,128)S(1)} %get-tuple-element.24.unit_ref, bf16[512,8192]{1,0:T(8,128)(2,1)S(1)} %copy-done), custom_call_target="tpu_custom_call" | custom-call | flops 2000000000 | bytes 16777216 | tf_op jit(solution)/shard_map/block_product/pallas_call | solution.py:228
  18.6 0.0 collective-permute-done
  18.7 19.8 %all_to_all.11.parts_ref = bf16[8,112,128]{2,1,0:T(8,128)(2,1)S(1)} all-to-all(bf16[8,112,128]{2,1,0:T(8,128)(2,1)S(1)} %broadcast_dynamic-update-slice_fusion), channel_id=1, replica_groups=mesh['row'=32,'col'=8] {'col'}, dimensions={0} | all-to-all | bytes 458752 | tf_op jit(solution)/shard_map/all_to_all | solution.py:242
  38.5 0.9 %scale_and_add.1 = f32[16,512]{1,0:T(8,128)} custom-call(bf16[8,112,128]{2,1,0:T(8,128)(2,1)S(1)} %all_to_all.11.parts_ref), custom_call_target="tpu_custom_call" | custom-call | tf_op jit(solution)/shard_map/scale_and_add/pallas_call | solution.py:243
  (3 shorter events, 0.0 us)
Async XLA Ops:
  0.0 16.3 %copy-start = (bf16[512,8192]{1,0:T(8,128)(2,1)S(1)}, bf16[512,8192]{1,0:T(8,128)(2,1)}, u32[]{:S(2)}) copy-start(bf16[512,8192]{1,0:T(8,128)(2,1)} %rows_ref.1) | copy-start | bytes 25165828
  13.7 4.9 %collective-permute-start = (f32[8,128]{1,0:T(8,128)S(1)}, f32[8,128]{1,0:T(8,128)S(1)}, u32[]{:S(2)}, u32[]{:S(2)}) collective-permute-start(f32[8,128]{1,0:T(8,128)S(1)} %get-tuple-element.26), channel_id=1, source_target_pairs={{0,192},{8,200},{16,208},{24,216},{32,224},{40,232},{48,240},{56,2... | collective-permute-start | bytes 12296 | tf_op jit(solution)/shard_map/ppermute | solution.py:226

commit v8 on v7

--- a/solution.py
+++ b/solution.py
@@ -98,9 +98,12 @@
     for t in range(tiles):
         norm = norm + line_ref[t : t + 1, :] * squares_ref[:, t * LANES : (t + 1) * LANES]
     lane = lax.broadcasted_iota(jnp.int32, (panel, LANES), 1)
-    norm = jnp.where(lane == 0, jnp.sum(norm, axis=1, keepdims=True), 0.0).T[0:SUBLANES]
-    norm_ref[...] = norm
-    sums_ref[...] = norm + flags_ref[...]
+    norm = jnp.where(lane == 0, jnp.sum(norm, axis=1, keepdims=True), 0.0).T[0:1]
+    high = norm.astype(jnp.bfloat16).astype(jnp.float32)
+    row = lax.broadcasted_iota(jnp.int32, norm_ref.shape, 0)
+    norm_ref[...] = jnp.where(row == 3, high, jnp.where(row == 4, norm - high, 0.0)).astype(norm_ref.dtype)
+    flags = jnp.concatenate([flags_ref[...], jnp.zeros_like(flags_ref[...])])
+    sums_ref[...] = jnp.where(row == 0, high, jnp.where(row == SUBLANES, norm - high, flags)).astype(sums_ref.dtype)
 
 
 def product_kernel(kept_ref, shifts_ref, poles_ref, unit_ref, rows_ref, out_ref):
@@ -146,7 +149,8 @@
     extra = (blocks + LOW_BLOCKS) * per_group
     rows = parts_ref[:, extra:, :].astype(jnp.float32)
     total = jnp.sum(rows, axis=0)
-    norm2, own, other = total[0:1] + total[SUBLANES : SUBLANES + 1], total[1:2], total[2:3]
+    norm2 = (total[0:1] + total[3:4]) + (total[4:5] + total[SUBLANES : SUBLANES + 1])
+    own, other = total[1:2], total[2:3]
     scale = jnp.where(other > 0.5, 0.0, 1.0 / jnp.sqrt(norm2))
     weights = [jnp.where(own > 0.5, rows[group, 1:2], scale) for group in range(groups)]
     columns_ref[...] = jnp.concatenate(weights, axis=0).T
@@ -215,7 +219,7 @@
     lines = lax.all_to_all(lines, "row", 0, 0, axis_index_groups=halves)
     norm, sums, kept = pl.pallas_call(
         norm_kernel,
-        out_shape=(row_struct, row_struct, line_struct(jnp.float32)),
+        out_shape=(struct((ALIGN, panel), jnp.bfloat16),) * 2 + (line_struct(jnp.float32),),
         in_specs=[vmem] * 5,
         out_specs=(vmem,) * 3,
         scratch_shapes=[pltpu.VMEM((tiles, LANES), jnp.float32)],
@@ -234,10 +238,7 @@
         cost_estimate=pl.CostEstimate(flops=2 * 10**9, bytes_accessed=2**24, transcendentals=2**20),
         name="block_product",
     )(kept, own_shifts, poles, unit, eigvec_rows)
-    norms = sums + other
-    first = lax.reduce_precision(norms, 8, 7)
-    extra = jnp.concatenate([first, norms - first]).astype(jnp.bfloat16)
-    extra = jnp.broadcast_to(extra, (col_count, ALIGN, LANES))
+    extra = jnp.broadcast_to(sums + other, (col_count, ALIGN, LANES))
     parts = lax.dynamic_update_slice(parts, extra, (0, body, 0))
     parts = lax.all_to_all(parts, "col", 0, 0)
     return pl.pallas_call(

time: 39.5 us -> 39.5 us (level)
  no operation moved by 1% of the time
where the time goes in v8:
time: 39.5 us; the launch traced here: 39.3 us
  blocking collectives  31 us (78%)
  Pallas kernels  5.67 us (14%)
  starting transfers between devices  2.57 us (7%)
    all_to_all x1, blocking collectives, local(): parts = lax.all_to_all(parts, 'col', 0, 0)  19.8 us
    all_to_all x1, blocking collectives, local(): lines = lax.all_to_all(lines, 'row', 0, 0, axis_index_groups=halves)  11.2 us
    ppermute x1, starting transfers between devices, local(): other = lax.ppermute(norm, 'row', [(i, i ^ flip) for i in range(row_count)])  2.57 us
    pallas_call x1, Pallas kernels, local(): pl.pallas_call(product_kernel, out_shape=struct((col_count, body + ALIGN,...  2.36 us
    pallas_call x1, Pallas kernels, local(): pl.pallas_call(functools.partial(pick_kernel, columns=width * col_count),...  1.99 us
    pallas_call x1, Pallas kernels, local(): pl.pallas_call(finish_kernel, out_shape=struct((panel // col_count, heigh...  0.86 us
  transfers between devices with their start and end apart: 1, of which 0 were waited for; matrix products, arithmetic and copies ran while one was open for 0% of the time, Pallas kernels for 6%

profile of v8, /device:TPU:8, one launch (start us, length us, event | category | flops | bytes accessed | tf_op | source)
XLA Modules:
  0.0 39.3 jit_solution(18331379320059363846)
XLA Ops:
  0.0 0.0 copy-start
  0.0 2.0 %pick_line.1 = (bf16[16,64,128]{2,1,0:T(8,128)(2,1)S(1)}, s32[64,128]{1,0:T(8,128)S(1)}, f32[64,128]{1,0:T(8,128)S(1)}, f32[128,128]{1,0:T(8,128)S(1)}, s32[128,...) custom-call(s32[2]{0:T(128)} %split_hbm.1, ...), custom_call_target="tpu_custom_call" | custom-call | tf_op jit(solution)/shard_map/pick_line/pallas_call | solution.py:192
  2.0 11.2 %all_to_all.10.lines_ref = bf16[16,64,128]{2,1,0:T(8,128)(2,1)S(1)} all-to-all(bf16[16,64,128]{2,1,0:T(8,128)(2,1)S(1)} %get-tuple-element.17), channel_id=1, replica_groups={{0,8,16,24,32,40,48,56,64,72,80,88,96,104,112,120},{128,136,144,152,160..., dimensions={0} | all-to-all | bytes 524288 | tf_op jit(solution)/shard_map/all_to_all | solution.py:219
  13.2 0.5 %column_norms.1 = (bf16[16,128]{1,0:T(8,128)(2,1)S(1)}, bf16[16,128]{1,0:T(8,128)(2,1)S(1)}, f32[64,128]{1,0:T(8,128)S(1)}) custom-call(f32[16,128]{1,0:T(8,128)S(1)} %get-tuple-element.16.holder_ref, bf16[16,64,128]{2,1,0:T(8,128)(2,1)S(1)} %all_to_all.10.lines_ref, s32[64,128]{1,0:T(8,128)S(1)} %get-tuple-element.18.mask_ref, ...), custom_call_target="tpu_custom_call" | custom-call | tf_op jit(solution)/shard_map/column_norms/pallas_call | solution.py:220
  13.7 2.6 %collective-permute-start = (bf16[16,128]{1,0:T(8,128)(2,1)S(1)}, bf16[16,128]{1,0:T(8,128)(2,1)S(1)}, u32[]{:S(2)}, u32[]{:S(2)}) collective-permute-start(bf16[16,128]{1,0:T(8,128)(2,1)S(1)} %get-tuple-element.26), channel_id=1, source_target_pairs={{0,192},{8,200},{16,208},{24,216},{32,224},{40,232},{48,240},{56,2... | collective-permute-start | bytes 12296 | tf_op jit(solution)/shard_map/ppermute | solution.py:230
  16.3 0.0 copy-done
  16.3 2.4 %block_product.1 = bf16[8,112,128]{2,1,0:T(8,128)(2,1)S(1)} custom-call(f32[64,128]{1,0:T(8,128)S(1)} %get-tuple-element.21.kept_ref, f32[64,128]{1,0:T(8,128)S(1)} %get-tuple-element.22.shifts_ref, f32[128,128]{1,0:T(8,128)S(1)} %get-tuple-element.23.poles_ref, s32[128,128]{1,0:T(8,128)S(1)} %get-tuple-element.24.unit_ref, bf16[512,8192]{1,0:T(8,128)(2,1)S(1)} %copy-done), custom_call_target="tpu_custom_call" | custom-call | flops 2000000000 | bytes 16777216 | tf_op jit(solution)/shard_map/block_product/pallas_call | solution.py:232
  18.7 0.0 collective-permute-done
  18.7 19.8 %all_to_all.11.parts_ref = bf16[8,112,128]{2,1,0:T(8,128)(2,1)S(1)} all-to-all(bf16[8,112,128]{2,1,0:T(8,128)(2,1)S(1)} %broadcast_dynamic-update-slice_fusion), channel_id=1, replica_groups=mesh['row'=32,'col'=8] {'col'}, dimensions={0} | all-to-all | bytes 458752 | tf_op jit(solution)/shard_map/all_to_all | solution.py:243
  38.5 0.9 %scale_and_add.1 = f32[16,512]{1,0:T(8,128)} custom-call(bf16[8,112,128]{2,1,0:T(8,128)(2,1)S(1)} %all_to_all.11.parts_ref), custom_call_target="tpu_custom_call" | custom-call | tf_op jit(solution)/shard_map/scale_and_add/pallas_call | solution.py:244
  (2 shorter events, 0.0 us)
Async XLA Ops:
  0.0 16.3 %copy-start = (bf16[512,8192]{1,0:T(8,128)(2,1)S(1)}, bf16[512,8192]{1,0:T(8,128)(2,1)}, u32[]{:S(2)}) copy-start(bf16[512,8192]{1,0:T(8,128)(2,1)} %rows_ref.1) | copy-start | bytes 25165828
  13.7 5.0 %collective-permute-start = (bf16[16,128]{1,0:T(8,128)(2,1)S(1)}, bf16[16,128]{1,0:T(8,128)(2,1)S(1)}, u32[]{:S(2)}, u32[]{:S(2)}) collective-permute-start(bf16[16,128]{1,0:T(8,128)(2,1)S(1)} %get-tuple-element.26), channel_id=1, source_target_pairs={{0,192},{8,200},{16,208},{24,216},{32,224},{40,232},{48,240},{56,2... | collective-permute-start | bytes 12296 | tf_op jit(solution)/shard_map/ppermute | solution.py:230
